TPU v7x, 128 devices: a whole 4x4x4 slice. The times are simulated.
128 devices in a mesh: member: 4 (over x_lo, core), space: 32 (over y, z, x_hi).
Axes of the slice: x: 4 (x_hi: 2, x_lo: 2; x = x_hi * 2 + x_lo), y: 4, z: 4, core: 2. Of those that a mesh axis runs over, the one named last changes fastest.
Arguments:
- latent: bfloat16 [16, 512, 1024], P('member', 'space'), may hold values from -6 to 6
- edge_index: int32 [3, 4096], P(None, 'space'), may hold values from 0 to 23, as said below
- edge_weight: float32 [3, 4096], P(None, 'space'), may hold values from 0.25 to 1
- noise_seed: int32 [16], P('member'), may hold values from 0 to 63
- noise_table: float32 [64, 1024], replicated, may hold values from -1.5 to 1.5
- w_in: bfloat16 [1024, 4096], P('space'), may hold values from -0.1875 to 0.1875
- w_out: bfloat16 [100, 4096], replicated, may hold values from -0.09375 to 0.09375
- target: float32 [100, 4096], P(None, 'space'), may hold values from -5 to 5
- area_weight: float32 [4096], P('space'), may hold values from 1 to 30, as said below
Outputs:
- loss: float32 [], replicated
- grad_latent: float32 [16, 512, 1024], P('member', 'space')
- grad_w_in: float32 [1024, 4096], P('space')
- grad_w_out: float32 [100, 4096], replicated
Inputs may be any that keep to these rules, and one draw needn't show every extreme that they name: `edge_index`: entry [k, p] indexes the extended block of the shard that holds point p: rows below 4 are the last 4 nodes of the previous shard, the next 16 rows its own nodes, the last 4 rows the first nodes of the next shard. Every edge lies within 4 nodes of the point's own node. `area_weight`: Positive.
All inputs are finite; a program needn't handle non-finite values.
Results may differ from a plain program's by a relative error of at most 0.0036.
The roundings to bfloat16 on the way count: a program that leaves them out, or rounds other values in their place, can miss the bound.
Values may be sent and summed in bfloat16 or wider, within the bound.
A program may use at most 128 MiB of HBM per device.

v0:
```python
from functools import partial

import jax
import jax.numpy as jnp
from jax import lax
from jax.sharding import PartitionSpec as P

VARS = 100
HALO = 4


epsilon = 1e-05
smoothing_sq = 0.04
loss_scale = 1024.0


def padded(x, sides, width):
    for axis, dim in sides:
        count, length = (lax.axis_size(axis), x.shape[dim])
        up = [(i, (i + 1) % count) for i in range(count - 1)]
        down = [(j, i) for i, j in up]
        last = lax.slice_in_dim(x, length - width, length, axis=dim)
        first = lax.slice_in_dim(x, 0, width, axis=dim)
        before = lax.ppermute(last, axis, up)
        after = lax.ppermute(first, axis, down)
        x = jnp.concatenate([before, x, after], axis=dim)
    return x


def normalize(aggregate, member_scale):
    average = jnp.mean(aggregate, axis=-1, keepdims=True)
    centred = aggregate - average
    spread = jnp.mean(centred * centred, axis=-1, keepdims=True)
    return centred * lax.rsqrt(spread + epsilon) * member_scale[:, None, :]


def smooth_abs(difference):
    return jnp.sqrt(difference * difference + smoothing_sq)


def smooth_slope(difference):
    return difference * lax.rsqrt(difference * difference + smoothing_sq)


def build_table(edge_index, edge_weight, ext_rows):
    node_ids = lax.broadcasted_iota(jnp.int32, (1, 1, ext_rows), 2)
    matches = jnp.where(
        edge_index[:, :, None] == node_ids,
        edge_weight[:, :, None],
        jnp.zeros((), edge_weight.dtype),
    )
    return jnp.sum(matches, axis=0)


def pair_sums(mine, others, totals):
    abs_sum, sign_sum = totals
    for member_row in range(others.shape[0]):
        difference = mine - others[member_row][None]
        abs_sum = abs_sum + smooth_abs(difference)
        sign_sum = sign_sum + smooth_slope(difference)
    return (abs_sum, sign_sum)


def local(
    latent, edge_index, edge_weight, noise_seed, noise_table, w_in, w_out, target, area_weight
):
    highest = lax.Precision.HIGHEST
    local_members = latent.shape[0]
    node_rows = latent.shape[1]
    members = lax.axis_size("member") * local_members
    points_all = lax.axis_size("space") * target.shape[1]
    pair_norm = 1.0 / (members * (members - 1))
    extended = padded(latent, (("space", 1),), HALO)
    ext_rows = extended.shape[1]
    weights_table = build_table(edge_index, edge_weight, ext_rows)
    aggregate = jnp.einsum(
        "pe,med->mpd", weights_table, extended.astype(jnp.float32), precision=highest
    )
    seed_hits = (
        noise_seed[:, None] == lax.broadcasted_iota(jnp.int32, (1, noise_table.shape[0]), 1)
    ).astype(jnp.float32)
    member_scale = 1.0 + jnp.dot(seed_hits, noise_table, precision=highest)
    normed = normalize(aggregate, member_scale).astype(jnp.bfloat16)
    w_whole = lax.all_gather(w_in, "space", axis=0, tiled=True)
    pre_act = jnp.einsum("mpd,dh->mph", normed, w_whole, preferred_element_type=jnp.float32)
    hidden = jax.nn.gelu(pre_act).astype(jnp.bfloat16)
    fields = jnp.einsum("mph,vh->mvp", hidden, w_out, preferred_element_type=jnp.float32)
    abs_pairs, sign_pairs = pair_sums(
        fields,
        lax.all_gather(fields, "member", axis=0, tiled=True),
        (jnp.zeros_like(fields), jnp.zeros_like(fields)),
    )
    misfit = fields - target[None]
    weighted = area_weight[None, None, :] / VARS
    local_loss = jnp.sum(weighted * (smooth_abs(misfit) / members - 0.5 * pair_norm * abs_pairs))
    grad_fields = (
        loss_scale * weighted * (smooth_slope(misfit) / members - pair_norm * sign_pairs)
    ).astype(jnp.bfloat16)
    grad_out_part = jnp.einsum(
        "mph,mvp->vh", hidden, grad_fields, preferred_element_type=jnp.float32
    )
    grad_hidden = jnp.einsum("mvp,vh->mph", grad_fields, w_out, preferred_element_type=jnp.float32)
    unused, gelu_back = jax.vjp(jax.nn.gelu, pre_act)
    grad_pre = gelu_back(grad_hidden)[0].astype(jnp.bfloat16)
    grad_normed = jnp.einsum("mph,dh->mpd", grad_pre, w_whole, preferred_element_type=jnp.float32)
    unused2, norm_back = jax.vjp(partial(normalize, member_scale=member_scale), aggregate)
    grad_aggregate = norm_back(grad_normed)[0]
    grad_window = jnp.einsum("pe,mpd->med", weights_table, grad_aggregate, precision=highest)
    edge_rims = jnp.concatenate([grad_window[:, :HALO], grad_window[:, HALO + node_rows :]], axis=1)
    arrived = padded(edge_rims, (("space", 1),), HALO)
    grad_latent = grad_window[:, HALO : HALO + node_rows]
    grad_latent = grad_latent.at[:, :HALO].add(arrived[:, :HALO])
    grad_latent = grad_latent.at[:, node_rows - HALO :].add(arrived[:, 3 * HALO :])
    total_loss, grad_out = lax.psum((local_loss, grad_out_part), ("member", "space"))
    flat_normed = normed.reshape(-1, normed.shape[2])
    flat_pre = grad_pre.reshape(-1, grad_pre.shape[2])
    grad_in_part = jnp.einsum(
        "rd,rh->dh", flat_normed, flat_pre, preferred_element_type=jnp.float32
    )
    space_count = lax.axis_size("space")
    member_count = lax.axis_size("member")
    piece_rows = grad_in_part.shape[0] // (space_count * member_count)
    reordered = grad_in_part.reshape(space_count, member_count, piece_rows, grad_in_part.shape[1])
    reordered = jnp.transpose(reordered, (1, 0, 2, 3)).reshape(grad_in_part.shape)
    own_piece = lax.psum_scatter(reordered, ("member", "space"), scatter_dimension=0, tiled=True)
    grad_in = lax.all_gather(own_piece, "member", axis=0, tiled=True)
    return (total_loss / points_all, grad_latent, grad_in / loss_scale, grad_out / loss_scale)


def solution(mesh):
    return jax.shard_map(
        local,
        mesh=mesh,
        in_specs=(
            P("member", "space", None),
            P(None, "space"),
            P(None, "space"),
            P("member"),
            P(),
            P("space", None),
            P(),
            P(None, "space"),
            P("space"),
        ),
        out_specs=(P(), P("member", "space", None), P("space", None), P()),
        check_vma=False,
    )
```

profile of v0, /device:TPU:1, one launch (start us, length us, event | category | flops | bytes accessed | tf_op | source)
XLA Modules:
  0.0 1033.3 jit_solution(16400809758389112549)
XLA Ops:
  7.2 0.0 copy-start
  7.2 0.0 all-gather.2.cloned.1.call-start
  7.2 0.7 all-gather.2.cloned.1.call-update
  7.9 0.0 all-reduce.2.cloned.1.call-start
  8.0 0.9 fusion.34
  8.9 5.5 collective-permute-start
  14.4 1.3 collective-permute-start.1
  15.7 1.2 broadcast_multiply_fusion.3
  16.9 1.2 convolution_add_fusion
  18.1 0.7 select_reduce_fusion
  18.8 1.7 collective-permute-done.1
  20.5 2.3 bitcast_reduce_fusion
  22.8 0.3 multiply_reduce_fusion.1
  23.2 1.4 multiply_convert_fusion.1
  24.6 2.3 copy.18
  26.9 90.9 %all-gather.2.cloned.1.call-done = bf16[1024,4096]{1,0:T(8,128)(2,1)} async-done(((bf16[32,4096]{1,0:T(8,128)(2,1)}), bf16[1024,4096]{1,0:T(8,128)(2,1)}) %all-gather.2.cloned.1.call-update) | async-done | bytes 8388624 | tf_op jit(solution)/shard_map/all_gather | solution.py:84
  117.8 13.0 %multiply_convert_fusion = (bf16[4,128,4096]{2,1,0:T(8,128)(2,1)S(1)}, f32[4,128,4096]{2,1,0:T(8,128)}) fusion(bf16[4,128,1024]{2,1,0:T(8,128)(2,1)} %multiply_convert_fusion.1, bf16[1024,4096]{1,0:T(8,128)(2,1)} %all-gather.2.cloned.1.call-done), kind=kOutput, calls=%fused_computation.14 | convolution fusion | flops 4313841664 | bytes 22020096 | tf_op jit(solution)/shard_map/mpd,dh->mph/dot_general | solution.py:85
  130.8 1.4 convolution_bitcast_fusion.2
  132.3 9.3 all_gather.10
  141.5 0.1 slice_bitcast_fusion.15
  141.8 0.5 copy-done.20
  142.2 0.0 copy-done.22
  142.3 0.0 copy-done.24
  142.3 0.0 copy-done.26
  142.3 0.0 copy-done.28
  142.3 0.0 copy-done.30
  142.4 0.0 copy-done.34
  142.4 0.0 copy-done.36
  142.4 2.7 convolution_bitcast_fusion.1
  145.1 10.7 %fusion.6 = bf16[4,128,4096]{2,1,0:T(8,128)(2,1)} fusion(f32[4,128,4096]{2,1,0:T(8,128)} %get-tuple-element.53, bf16[100,4096]{1,0:T(8,128)(2,1)S(1)} %copy-done, f32[4,100,128]{2,1,0:T(8,128)S(1)} %convolution_bitcast_fusion.2, f32[128]{0:T(128)} %get-tuple-element.48, f32[100,128]{1,0:T(8,128)S(1)} %get-tuple-element.29, ...), kind=kOutput, calls=%fused_computation.9 | convolution fusion | flops 465879040 | bytes 14477824 | tf_op jit(solution)/shard_map/mvp,vh->mph/dot_general | solution.py:102
  155.8 0.0 all-reduce.2.cloned.1.call-update
  155.9 0.3 reduce-scatter.2.cloned.1.call-start
  156.1 6.6 convolution_bitcast_fusion
  162.7 6.1 copy.19
  168.8 0.0 reduce-scatter.2.cloned.1.call-update
  168.9 8.5 multiply_reduce_fusion
  177.6 0.7 fusion.19
  178.3 2.8 fusion.13
  181.1 3.6 collective-permute-start.2
  184.8 1.9 multiply_reduce_fusion.2
  186.8 65.3 %psum.14 = f32[]{:T(128)} all-reduce(f32[]{:T(128)} %multiply_reduce_fusion.2), channel_id=1, replica_groups=mesh['member'=4,'space'=32] {'member','space'}, use_global_device_ids=true, to_apply=%region_4.5 | all-reduce | flops 1 | bytes 8 | tf_op jit(solution)/shard_map/psum | solution.py:114
  252.1 1.3 collective-permute-start.3
  254.1 4.5 collective-permute-done.3
  258.7 46.6 %all-reduce.2.cloned.1.call-done = f32[100,4096]{1,0:T(8,128)} async-done(((f32[100,4096]{1,0:T(8,128)}), f32[100,4096]{1,0:T(8,128)}) %all-reduce.2.cloned.1.call-update) | async-done | bytes 1638416 | tf_op jit(solution)/shard_map/psum | solution.py:114
  305.3 2.8 broadcast_multiply_fusion
  308.1 703.6 %reduce-scatter.2.cloned.1.call-done = f32[8,4096]{1,0:T(8,128)} async-done(((f32[1024,4096]{1,0:T(8,128)}), f32[8,4096]{1,0:T(8,128)}) %reduce-scatter.2.cloned.1.call-update) | async-done | bytes 131088 | tf_op jit(solution)/shard_map/reduce_scatter | solution.py:125
  1011.7 13.1 %all_gather.11 = f32[32,4096]{1,0:T(8,128)S(1)} all-gather(f32[8,4096]{1,0:T(8,128)} %reduce-scatter.2.cloned.1.call-done), channel_id=1, replica_groups=mesh['member'=4,'space'=32] {'member'}, dimensions={0}, use_global_device_ids=true | all-gather | bytes 655360 | tf_op jit(solution)/shard_map/all_gather | solution.py:126
  1024.8 0.8 broadcast_multiply_fusion.1
  (95 shorter events, 0.4 us)
Async XLA Ops:
  7.2 123.7 %copy-start = (bf16[100,4096]{1,0:T(8,128)(2,1)S(1)}, bf16[100,4096]{1,0:T(8,128)(2,1)}, u32[]{:S(2)}) copy-start(bf16[100,4096]{1,0:T(8,128)(2,1)} %param.19) | copy-start | bytes 2457604
  7.2 110.6 %all-gather.2.cloned.1.call-start = ((), (), s32[]{:S(2)}) async-start(), calls=%async_computation.1 | async-start | bytes 8650752 | tf_op jit(solution)/shard_map/all_gather | solution.py:84
  7.9 297.4 %all-reduce.2.cloned.1.call-start = ((), (), s32[]{:S(2)}) async-start(), calls=%async_computation.3 | async-start | bytes 3407872 | tf_op jit(solution)/shard_map/psum | solution.py:114
  8.9 9.9 collective-permute-start
  14.4 6.2 collective-permute-start.1
  18.1 159.3 %copy-start.3 = (f32[4,1024]{1,0:T(4,128)}, f32[4,1024]{1,0:T(4,128)S(1)}, u32[]{:S(2)}) copy-start(f32[4,1024]{1,0:T(4,128)S(1)} %convolution_add_fusion) | copy-start | bytes 49156
  18.8 8.1 copy-start.4
  22.8 154.6 %copy-start.38 = (f32[4,128]{1,0:T(4,128)}, f32[4,128]{1,0:T(4,128)S(1)}, u32[]{:S(2)}) copy-start(f32[4,128]{1,0:T(4,128)S(1)} %broadcast_multiply_fusion.2) | copy-start | bytes 6148
  23.2 107.6 %copy-start.41 = (f32[4,128]{1,0:T(4,128)}, f32[4,128]{1,0:T(4,128)S(1)}, u32[]{:S(2)}) copy-start(f32[4,128]{1,0:T(4,128)S(1)} %multiply_reduce_fusion.1) | copy-start | bytes 6148
  23.2 107.6 %copy-start.39 = (f32[4,128]{1,0:T(4,128)}, f32[4,128]{1,0:T(4,128)S(1)}, u32[]{:S(2)}) copy-start(f32[4,128]{1,0:T(4,128)S(1)} %fusion.30) | copy-start | bytes 6148
  130.8 11.6 %copy-start.43 = (f32[100,128]{1,0:T(8,128)S(1)}, f32[100,128]{1,0:T(8,128)}, u32[]{:S(2)}) copy-start(f32[100,128]{1,0:T(8,128)} %param.20) | copy-start | bytes 153604
  130.8 11.6 %copy-start.46 = (f32[128]{0:T(128)S(1)}, f32[128]{0:T(128)}, u32[]{:S(2)}) copy-start(f32[128]{0:T(128)} %get-tuple-element.48) | copy-start | bytes 1540
  141.7 0.7 copy-start.30
  141.7 0.7 copy-start.34
  141.7 0.7 copy-start.36
  141.7 3.4 copy-start.6
  141.7 3.4 copy-start.8
  141.7 3.4 copy-start.10
  141.7 3.4 copy-start.12
  141.7 3.4 copy-start.14
  141.7 3.4 copy-start.16
  141.8 3.4 copy-start.18
  155.9 855.8 %reduce-scatter.2.cloned.1.call-start = ((), (), s32[]{:S(2)}) async-start(), calls=%async_computation.2 | async-start | bytes 16908288 | tf_op jit(solution)/shard_map/reduce_scatter | solution.py:125
  168.8 8.5 copy-start.42
  168.9 8.5 copy-start.40
  177.3 1.0 copy-start.5
  177.4 7.3 copy-start.7
  177.4 7.3 copy-start.9
  177.4 7.3 copy-start.11
  177.4 7.3 copy-start.13
  177.5 7.3 copy-start.15
  177.5 7.3 copy-start.17
  177.5 7.3 copy-start.19
  177.5 7.3 copy-start.21
  177.5 7.3 copy-start.23
  177.5 7.3 copy-start.25
  177.5 7.3 copy-start.27
  177.5 7.3 copy-start.29
  177.5 7.3 copy-start.31
  177.5 7.3 copy-start.33
  177.6 7.3 copy-start.35
  177.6 7.3 copy-start.37
  177.6 7.3 copy-start.44
  177.6 7.2 copy-start.45
  178.3 847.3 %copy-start.1 = (bf16[100,4096]{1,0:T(8,128)(2,1)S(1)}, bf16[100,4096]{1,0:T(8,128)(2,1)}, u32[]{:S(2)}) copy-start(bf16[100,4096]{1,0:T(8,128)(2,1)} %param.19) | copy-start | bytes 2457604
  181.1 73.0 %collective-permute-start.2 = (f32[4,4,1024]{2,1,0:T(4,128)S(1)}, f32[4,4,1024]{2,1,0:T(4,128)S(1)}, u32[]{:S(2)}, u32[]{:S(2)}) collective-permute-start(f32[4,4,1024]{2,1,0:T(4,128)S(1)} %get-tuple-element.45), channel_id=1, source_target_pairs={{0,1},{1,2},{2,3},{3,4},{4,5},{5,6},{6,7},{7,8},{8,9},{9,10},{10,1... | collective-permute-start | bytes 196616 | tf_op jit(solution)/shard_map/ppermute | solution.py:24
  252.1 6.5 collective-permute-start.3
  258.7 767.0 %copy-start.2 = (f32[4,16,1024]{2,1,0:T(8,128)}, f32[4,16,1024]{2,1,0:T(8,128)S(1)}, u32[]{:S(2)}) copy-start(f32[4,16,1024]{2,1,0:T(8,128)S(1)} %fusion.26) | copy-start | bytes 786436
  (6 other events, 3.9 us)
Sparse Core Ops, SparseCore 0:
  11.2 106.6 all-gather.1
  156.0 149.2 all-reduce.1
  307.7 703.9 reduce-scatter.1
where the time goes:
time: 1030 us
  waiting for transfers between devices  848 us (82%)
  blocking collectives  87.7 us (9%)
  matrix products  49.1 us (5%)
  between operations  16.3 us (2%)
  starting transfers between devices  12 us (1%)
    reduce_scatter x1, waiting for transfers between devices, local(): lax.psum_scatter(reordered, ('member', 'space'), scatter_dimension=0, til...  704 us
    all_gather x1, waiting for transfers between devices, local(): w_whole = lax.all_gather(w_in, 'space', axis=0, tiled=True)  90.9 us
    psum x1, blocking collectives, local(): lax.psum((local_loss, grad_out_part), ('member', 'space'))  65.3 us
    psum x1, waiting for transfers between devices, local(): lax.psum((local_loss, grad_out_part), ('member', 'space'))  46.6 us
  transfers between devices with their start and end apart: 7, of which 5 were waited for; matrix products, arithmetic and copies ran while one was open for 4% of the time, Pallas kernels for 0%

commit v1 on v0

v1 whole, which is shorter than its diff:
```python
import jax
import jax.numpy as jnp
from jax import lax
from jax.experimental import pallas as pl
from jax.experimental.pallas import tpu as pltpu
from jax.sharding import PartitionSpec as P

VARS = 100
HALO = 4
MEMBERS = 16
POINTS = 4096
F32 = jnp.float32
BF16 = jnp.bfloat16
EPS = 1e-05
SMOOTH = 0.04
SCALE = 1024.0
PAIR = 1.0 / (MEMBERS * (MEMBERS - 1))
GELU_C = 0.7978845608028654
MESH = pl.DeviceIdType.MESH

LAT = 1024
HALF = 2048
WIDE = HALF + 256
PARTS = [(0, 384), (384, 384), (768, 384), (1152, 384), (1536, 256), (1792, 256)]
ORDERS = ["yzx", "zxy", "xyz", "yxz", "zyx", "xzy"]
OUT_PARTS = [(2048, 128), (2176, 128)]
OUT_ORDERS = ["zyx", "xzy"]
ALL_PARTS = PARTS + OUT_PARTS
ALL_ORDERS = ORDERS + OUT_ORDERS

DMA = pltpu.SemaphoreType.DMA
SCRATCH = dict(
    wbuf=pltpu.VMEM((4, 4, 4, 16, HALF), BF16),
    wo=pltpu.VMEM((128, HALF), BF16),
    nbuf=pltpu.VMEM((8, 128, LAT), BF16),
    n_t=pltpu.VMEM((LAT, 1024), BF16),
    xhat=pltpu.VMEM((4, 128, LAT), F32),
    rstd=pltpu.VMEM((4, 128, 128), F32),
    tab=pltpu.VMEM((128, 128), F32),
    small=pltpu.VMEM((3, 128, 128), F32),
    hid=pltpu.VMEM((1024, HALF), BF16),
    big=pltpu.VMEM((4, 4, 4, 16, WIDE), F32),
    gpre=pltpu.VMEM((1024, HALF), BF16),
    halo_s=pltpu.VMEM((2, 16, LAT), BF16),
    halo_r=pltpu.VMEM((2, 16, LAT), BF16),
    fpart=pltpu.VMEM((8, 4, 32, 128), F32),
    fcore=pltpu.VMEM((8, 2, 32, 128), F32),
    fsum=pltpu.VMEM((2, 8, 32, 128), F32),
    fother=pltpu.VMEM((8, 32, 128), F32),
    gf=pltpu.VMEM((8, 4, 32, 128), BF16),
    gfo=pltpu.VMEM((8, 32, 128), BF16),
    gf_t=pltpu.VMEM((128, 1024), BF16),
    sb1=pltpu.VMEM((4, 4, 4, 16, WIDE), BF16),
    rb1=pltpu.VMEM((3, 4, 4, 16, WIDE), BF16),
    q1=pltpu.VMEM((4, 4, 16, WIDE), F32),
    sb2=pltpu.VMEM((4, 4, 16, WIDE), BF16),
    rb2=pltpu.VMEM((3, 4, 16, WIDE), BF16),
    q2=pltpu.VMEM((4, 16, WIDE), F32),
    sb3=pltpu.VMEM((4, 16, WIDE), BF16),
    rb3=pltpu.VMEM((3, 16, WIDE), BF16),
    fin=pltpu.VMEM((2, 2, 16, HALF), F32),
    obuf=pltpu.VMEM((2, 4, 4, 4, 16, 256), BF16),
    gno=pltpu.VMEM((4, 128, LAT), F32),
    gns=pltpu.VMEM((4, 128, LAT), BF16),
    gnr=pltpu.VMEM((4, 128, LAT), BF16),
    rim_s=pltpu.VMEM((2, 16, LAT), F32),
    rim_r=pltpu.VMEM((2, 16, LAT), F32),
    loss_s=pltpu.VMEM((4, 8, 128), F32),
    loss_r=pltpu.VMEM((10, 8, 128), F32),
    ag_ss=DMA((6, 3, 3)),
    ag_rs=DMA((6, 3, 3)),
    rs_ss=DMA((8, 3, 3)),
    rs_rs=DMA((8, 3, 3)),
    oa_ss=DMA((2, 3, 3)),
    oa_rs=DMA((2, 3, 3)),
    fin_ss=DMA((6, 3)),
    fin_rs=DMA((6, 3)),
    n_ss=DMA((4,)),
    n_rs=DMA((4,)),
    gn_ss=DMA((4,)),
    gn_rs=DMA((4,)),
    halo_ss=DMA((2,)),
    halo_rs=DMA((2,)),
    rim_ss=DMA((2,)),
    rim_rs=DMA((2,)),
    f_ss=DMA((2,)),
    f_rs=DMA((2,)),
    g_ss=DMA((3,)),
    g_rs=DMA((3,)),
    oc_ss=DMA,
    oc_rs=DMA,
    l_ss=DMA((10,)),
    l_rs=DMA((10,)),
)


def dot(a, b, dims=((1,), (0,)), precision=None):
    return lax.dot_general(a, b, (dims, ((), ())), precision=precision, preferred_element_type=F32)


class Place:
    def __init__(self):
        m, s = lax.axis_index("member"), lax.axis_index("space")
        self.m, self.s = m, s
        self.xl, self.core = m // 2, m % 2
        self.y, self.z, self.xh = s // 8, (s // 2) % 4, s % 2
        self.x = self.xh * 2 + self.xl

    def device(self, y, z, x):
        return ((x % 2) * 2 + self.core, (y * 4 + z) * 2 + x // 2)

    def at(self, axis):
        return getattr(self, axis)

    def peer(self, axis, step):
        q = dict(y=self.y, z=self.z, x=self.x)
        q[axis] = (q[axis] + step) % 4
        return self.device(**q)

    def core_peer(self):
        return (self.xl * 2 + 1 - self.core, self.s)

    def pair_peer(self):
        return ((1 - self.xl) * 2 + self.core, self.s)

    def cross_peer(self):
        return ((1 - self.xl) * 2 + 1 - self.core, self.s)

    def shard(self, step):
        return (self.m, (self.s + step + 32) % 32)


class Copies:
    def __init__(self):
        self.sent = []

    def send(self, src, dst, ss, rs, device):
        copy = pltpu.make_async_remote_copy(
            src_ref=src, dst_ref=dst, send_sem=ss, recv_sem=rs, device_id=device, device_id_type=MESH
        )
        copy.start()
        self.sent.append(copy)
        return copy

    def drain(self):
        for copy in self.sent:
            copy.wait_send()


def arrive(copies):
    for copy in copies:
        copy.wait_recv()


def kernel(lat, eidx, ewt, seed, ntab, w_in, w_out, target, area, loss_o, gl_o, gwi_o, gwo_o, *refs):
    r = dict(zip(SCRATCH, refs))
    wbuf, big, nbuf, n_t, hid, gpre, wo = (r[k] for k in ("wbuf", "big", "nbuf", "n_t", "hid", "gpre", "wo"))
    xhat, rstd, tab, small = r["xhat"], r["rstd"], r["tab"], r["small"]
    me = Place()
    c = Copies()
    col0 = pl.multiple_of(me.core * HALF, 128)

    friends = [me.peer(a, k) for a in "yzx" for k in (1, 2, 3)]
    friends += [me.core_peer(), me.cross_peer(), me.shard(1), me.shard(-1)]
    barrier = pltpu.get_barrier_semaphore()
    for d in friends:
        pl.semaphore_signal(barrier, inc=1, device_id=d, device_id_type=MESH)

    wbuf[me.y, me.z, me.x] = w_in[pl.ds(pl.multiple_of(me.xl * 16, 16), 16), pl.ds(col0, HALF)]
    lat32 = [lat[i].astype(F32) for i in range(4)]
    r["halo_s"][0] = jnp.concatenate([v[12:16] for v in lat32], axis=0).astype(BF16)
    r["halo_s"][1] = jnp.concatenate([v[0:4] for v in lat32], axis=0).astype(BF16)
    pl.semaphore_wait(barrier, len(friends))

    halo = [
        c.send(r["halo_s"].at[0], r["halo_r"].at[0], r["halo_ss"].at[0], r["halo_rs"].at[0], me.shard(1)),
        c.send(r["halo_s"].at[1], r["halo_r"].at[1], r["halo_ss"].at[1], r["halo_rs"].at[1], me.shard(-1)),
    ]

    gathered = {}

    def gather_stage(stage):
        for k, (c0, cw) in enumerate(PARTS):
            arrive(gathered.get(k, []))
            order = ORDERS[k]
            index = tuple(pl.ds(0, 4) if a in order[:stage] else pl.ds(me.at(a), 1) for a in "yzx")
            index += (slice(None), pl.ds(c0, cw))
            gathered[k] = [
                c.send(
                    wbuf.at[index], wbuf.at[index], r["ag_ss"].at[k, stage, i - 1], r["ag_rs"].at[k, stage, i - 1],
                    me.peer(order[stage], i),
                )
                for i in (2, 1, 3)
            ]

    gather_stage(0)

    node = lax.broadcasted_iota(jnp.int32, (128, 128), 0)
    row_of = jnp.where(node < 16, node + HALO, jnp.where(node < 20, node - 16, jnp.where(node < 24, node, -1)))
    table_t = jnp.zeros((128, 128), F32)
    for k in range(3):
        table_t = table_t + jnp.where(row_of == eidx[k : k + 1, :], ewt[k : k + 1, :], 0.0)
    tab[...] = table_t
    table = table_t.T[:, :32]
    t_hi = table.astype(BF16)
    t_rest = table - t_hi.astype(F32)
    t_mid = t_rest.astype(BF16)
    t_low = (t_rest - t_mid.astype(F32)).astype(BF16)
    small[0] = jnp.zeros((128, 128), F32)
    small[0, 0:VARS] = target[...]
    small[1] = small[0].T
    small[2] = jnp.broadcast_to(area[...], (128, 128)).T

    arrive(halo)
    has_prev = (me.s > 0).astype(F32)
    has_next = (me.s < 31).astype(F32)
    normed = []
    for i in range(4):
        prev = r["halo_r"][0].astype(F32)[4 * i : 4 * i + 4] * has_prev
        nxt = r["halo_r"][1].astype(F32)[4 * i : 4 * i + 4] * has_next
        window = jnp.concatenate([lat[i].astype(F32), prev, nxt, jnp.zeros((8, LAT), F32)], axis=0).astype(BF16)
        xhat[i] = dot(t_hi, window) + dot(t_mid, window) + dot(t_low, window)
        scale = 1.0 + ntab[pl.ds(seed[i], 1), :]
        row = me.core * 4 + i

        @pl.loop(0, 4)
        def _(j):
            rows = pl.ds(pl.multiple_of(j * 32, 32), 32)
            a = xhat[i, rows, :]
            centred = a - jnp.mean(a, axis=-1, keepdims=True)
            inv = lax.rsqrt(jnp.mean(centred * centred, axis=-1, keepdims=True) + EPS)
            unit = centred * inv
            xhat[i, rows, :] = unit
            rstd[i, rows, :] = jnp.broadcast_to(inv, (32, 128))
            nbuf[row, rows, :] = (unit * scale).astype(BF16)

        normed.append(c.send(nbuf.at[row], nbuf.at[row], r["n_ss"].at[i], r["n_rs"].at[i], me.core_peer()))
        if i == 1:
            gather_stage(1)

    big[0, 0:2, :, :, 0:HALF] = jnp.zeros((2, 4, 16, HALF), F32)
    head = w_out[:, pl.ds(col0, HALF)].astype(F32)
    for v in range(6):
        big[0, v // 4, v % 4, :, 0:HALF] = head[16 * v : 16 * v + 16]
    big[0, 1, 2, 0:4, 0:HALF] = head[96:100]
    wo[...] = big[0, 0:2, :, :, 0:HALF].reshape(128, HALF).astype(BF16)

    gather_stage(2)
    arrive(normed)
    for i in range(8):
        n_t[:, 128 * i : 128 * i + 128] = nbuf[i].T
    for k in range(6):
        arrive(gathered[k])

    @pl.loop(0, HALF // 256)
    def _(j):
        cols = pl.ds(pl.multiple_of(j * 256, 256), 256)
        w = wbuf[:, :, :, :, cols].reshape(LAT, 256)
        for h in range(4):
            pre = dot(nbuf[2 * h : 2 * h + 2].reshape(256, LAT), w)
            sq = pre * pre
            t = jnp.tanh(pre * (GELU_C + (GELU_C * 0.044715) * sq))
            cdf = 0.5 + 0.5 * t
            hid[256 * h : 256 * h + 256, cols] = (pre * cdf).astype(BF16)
            slope = cdf + (0.5 * pre) * (1.0 - t * t) * (GELU_C + (3.0 * GELU_C * 0.044715) * sq)
            big[h, :, :, :, cols] = slope.reshape(4, 4, 16, 256)

    for h in range(4):
        part = dot(hid[256 * h : 256 * h + 256, :], wo[...], ((1,), (1,)))
        r["fpart"][2 * h : 2 * h + 2] = part.reshape(2, 4, 32, 128)

    fpart, fcore, fsum, fother, gf, gfo = (r[k] for k in ("fpart", "fcore", "fsum", "fother", "gf", "gfo"))
    f1 = c.send(
        fpart.at[:, pl.ds(2 * (1 - me.core), 2)], fcore, r["f_ss"].at[0], r["f_rs"].at[0], me.core_peer()
    )
    f1.wait_recv()
    for g in range(2):
        fsum[g] = fpart[:, 2 * me.core + g] + fcore[:, g]
    f2 = c.send(fsum.at[1 - me.xl], fother, r["f_ss"].at[1], r["f_rs"].at[1], me.pair_peer())
    group = me.core * 2 + me.xl
    f2.wait_recv()

    r["loss_s"][0] = jnp.zeros((8, 128), F32)
    lane = lax.broadcasted_iota(jnp.int32, (8, 128), 1)

    @pl.loop(0, 4)
    def _(j):
        rows = pl.ds(pl.multiple_of(j * 8, 8), 8)
        point = pl.ds(pl.multiple_of(group * 32 + j * 8, 8), 8)
        f = [fsum[me.xl, i, rows, :] for i in range(8)] + [fother[i, rows, :] for i in range(8)]
        weighted = jnp.where(lane < VARS, small[2, point, :] / VARS, 0.0)
        goal = small[1, point, :]
        signs = [jnp.zeros((8, 128), F32) for _ in range(MEMBERS)]
        pairs = jnp.zeros((8, 128), F32)
        for a in range(MEMBERS):
            for b in range(a + 1, MEMBERS):
                d = f[a] - f[b]
                q = d * d + SMOOTH
                inv = lax.rsqrt(q)
                pairs = pairs + q * inv
                sl = d * inv
                signs[a] = signs[a] + sl
                signs[b] = signs[b] - sl
        misfits = jnp.zeros((8, 128), F32)
        for a in range(MEMBERS):
            d = f[a] - goal
            q = d * d + SMOOTH
            inv = lax.rsqrt(q)
            misfits = misfits + q * inv
            grad = (SCALE * weighted) * ((d * inv) * (1.0 / MEMBERS) - PAIR * signs[a])
            r["small_g"][a, rows, :] = grad
        term = misfits * (1.0 / MEMBERS) - PAIR * (pairs + MEMBERS * 0.5 * 0.2)
        r["loss_s"][0] += weighted * term

    for a in range(8):
        gf[a, group] = r["small_g"][a].astype(BF16)
        gfo[a] = r["small_g"][8 + a].astype(BF16)
    gs = [
        c.send(gfo, gf.at[:, group], r["g_ss"].at[0], r["g_rs"].at[0], me.pair_peer()),
        c.send(gfo, gf.at[:, group], r["g_ss"].at[1], r["g_rs"].at[1], me.cross_peer()),
        c.send(gf.at[:, group], gf.at[:, group], r["g_ss"].at[2], r["g_rs"].at[2], me.core_peer()),
    ]

    loss_s, loss_r = r["loss_s"], r["loss_r"]
    loss_pending = []

    def loss_send(level):
        if level == 0:
            loss_pending.append(
                [c.send(loss_s.at[0], loss_r.at[0], r["l_ss"].at[0], r["l_rs"].at[0], me.core_peer())]
            )
            return
        axis = "yzx"[level - 1]
        loss_pending.append(
            [
                c.send(
                    loss_s.at[level], loss_r.at[3 * level - 3 + i], r["l_ss"].at[3 * level - 3 + i],
                    r["l_rs"].at[3 * level - 3 + i], me.peer(axis, i),
                )
                for i in (1, 2, 3)
            ]
        )

    def loss_next(level):
        arrive(loss_pending[level])
        if level == 0:
            loss_s[1] = loss_s[0] + loss_r[0]
            return
        v = me.at("yzx"[level - 1])
        base = 3 * level - 3
        own, one, two, three = loss_s[level], loss_r[base + 1], loss_r[base + 2], loss_r[base + 3]
        total = (own + two) + (one + three)
        if level < 3:
            loss_s[level + 1] = total
        else:
            loss_o[...] = total

    loss_send(0)
    arrive(gs)
    gf_rows = gf[...].reshape(1024, 128)
    r["gf_t"][...] = gf_rows.T

    sb1, rb1, q1, sb2, rb2, q2, sb3, rb3, fin, obuf = (
        r[k] for k in ("sb1", "rb1", "q1", "sb2", "rb2", "q2", "sb3", "rb3", "fin", "obuf")
    )
    flight = {}

    def pick(axis, axes, value, cols):
        return tuple(value if a == axis else slice(None) for a in axes) + (slice(None), cols)

    def scatter_send(k, stage):
        c0, cw = ALL_PARTS[k]
        cols, order = pl.ds(c0, cw), ALL_ORDERS[k]
        axis = order[stage]
        axes = [a for a in "yzx" if a not in order[:stage]]
        src, dst = ((sb1, rb1), (sb2, rb2), (sb3, rb3))[stage]
        flight[k] = []
        for i in (2, 1, 3):
            there = (me.at(axis) + i) % 4
            flight[k].append(
                c.send(
                    src.at[pick(axis, axes, there, cols)],
                    dst.at[(i - 1,) + (slice(None),) * (3 - stage) + (cols,)],
                    r["rs_ss"].at[k, stage, i - 1], r["rs_rs"].at[k, stage, i - 1], me.peer(axis, i),
                )
            )

    def scatter_add(k, stage):
        c0, cw = ALL_PARTS[k]
        cols, order = slice(c0, c0 + cw), ALL_ORDERS[k]
        axis = order[stage]
        axes = [a for a in "yzx" if a not in order[:stage]]
        arrive(flight[k])
        own = (big, q1, q2)[stage]
        dst = (rb1, rb2, rb3)[stage]
        where = me.at(axis)
        if stage == 2:
            total = own[where, :, cols]
            for i in range(3):
                total = total + dst[i, :, cols].astype(F32)
            return total
        spot = axes.index(axis)
        keep, send = ((q1, sb2), (q2, sb3))[stage]
        for v in range(4):
            if stage == 0:
                index = [v, slice(None)]
                index.insert(spot, where)
                total = own[tuple(index) + (slice(None), cols)]
                for i in range(3):
                    total = total + dst[i, v, :, :, cols].astype(F32)
                keep[v, :, :, cols] = total
                send[v, :, :, cols] = total.astype(BF16)
            else:
                index = [v]
                index.insert(spot, where)
                total = own[tuple(index) + (slice(None), cols)]
                for i in range(3):
                    total = total + dst[i, v, :, cols].astype(F32)
                keep[v, :, cols] = total
                send[v, :, cols] = total.astype(BF16)

    def advance(k, stage):
        scatter_add(k, stage)
        scatter_send(k, stage + 1)

    finals = {}

    def finish(k):
        c0, cw = PARTS[k]
        total = scatter_add(k, 2) * (1.0 / SCALE)
        fin[me.xl, me.core, :, c0 : c0 + cw] = total
        here = fin.at[me.xl, me.core, :, pl.ds(c0, cw)]
        finals[k] = [
            c.send(here, here, r["fin_ss"].at[k, i], r["fin_rs"].at[k, i], d)
            for i, d in enumerate((me.pair_peer(), me.cross_peer(), me.core_peer()))
        ]

    out_flight = {}

    def out_stage(part, stage):
        order = ("yzx", "xyz")[part]
        c0 = 128 * part
        if stage == 0:
            total = scatter_add(6 + part, 2)
            obuf[me.core, me.y, me.z, me.x, :, c0 : c0 + 128] = total.astype(BF16)
        else:
            arrive(out_flight[part])
        if stage == 3:
            return
        index = (me.core,)
        index += tuple(pl.ds(0, 4) if a in order[:stage] else pl.ds(me.at(a), 1) for a in "yzx")
        index += (slice(None), pl.ds(c0, 128))
        out_flight[part] = [
            c.send(
                obuf.at[index], obuf.at[index], r["oa_ss"].at[part, stage, i - 1], r["oa_rs"].at[part, stage, i - 1],
                me.peer(order[stage], i),
            )
            for i in (2, 1, 3)
        ]

    for hg in range(8):
        part = dot(r["gf_t"][...], hid[:, 256 * hg : 256 * hg + 256])
        for vg in range(8):
            b = vg * 8 + hg
            block = part[16 * vg : 16 * vg + 16]
            big[b // 16, (b // 4) % 4, b % 4, :, HALF:WIDE] = block
            sb1[b // 16, (b // 4) % 4, b % 4, :, HALF:WIDE] = block.astype(BF16)
    scatter_send(6, 0)
    scatter_send(7, 0)

    def column_part(k):
        c0, cw = PARTS[k]
        cols = slice(c0, c0 + cw)
        for h in range(4):
            back = dot(gf[2 * h : 2 * h + 2].reshape(256, 128), wo[:, cols])
            slope = big[h, :, :, :, cols].reshape(256, cw)
            gpre[256 * h : 256 * h + 256, cols] = (back * slope).astype(BF16)
        for y in range(4):
            grad = dot(n_t[256 * y : 256 * y + 256, :], gpre[:, cols]).reshape(4, 4, 16, cw)
            big[y, :, :, :, cols] = grad
            sb1[y, :, :, :, cols] = grad.astype(BF16)
        scatter_send(k, 0)

    column_part(0)
    loss_next(0)
    loss_send(1)
    advance(6, 0)
    advance(7, 0)
    column_part(1)
    column_part(2)
    advance(0, 0)
    loss_next(1)
    loss_send(2)
    advance(6, 1)
    advance(7, 1)
    column_part(3)
    advance(1, 0)
    column_part(4)
    advance(2, 0)
    advance(0, 1)
    loss_next(2)
    loss_send(3)
    out_stage(0, 0)
    out_stage(1, 0)
    column_part(5)
    advance(3, 0)
    advance(1, 1)

    gno, gns, gnr = r["gno"], r["gns"], r["gnr"]
    theirs = pl.multiple_of((1 - me.core) * 512, 512)
    mine = pl.multiple_of(me.core * 512, 512)
    for n in range(4):
        part = dot(gpre[pl.ds(theirs, 512), :], wbuf[n].reshape(256, HALF), ((1,), (1,)))
        gns[:, :, 256 * n : 256 * n + 256] = part.reshape(4, 128, 256).astype(BF16)
    gn = [c.send(gns.at[i], gnr.at[i], r["gn_ss"].at[i], r["gn_rs"].at[i], me.core_peer()) for i in range(4)]
    advance(4, 0)
    advance(2, 1)
    out_stage(0, 1)
    out_stage(1, 1)
    finish(0)
    for n in range(4):
        part = dot(gpre[pl.ds(mine, 512), :], wbuf[n].reshape(256, HALF), ((1,), (1,)))
        gno[:, :, 256 * n : 256 * n + 256] = part.reshape(4, 128, 256)
    advance(5, 0)
    advance(3, 1)
    finish(1)
    out_stage(0, 2)
    out_stage(1, 2)

    for i in range(4):
        scale = 1.0 + ntab[pl.ds(seed[i], 1), :]
        gn[i].wait_recv()

        @pl.loop(0, 4)
        def _(j):
            rows = pl.ds(pl.multiple_of(j * 32, 32), 32)
            g = (gno[i, rows, :] + gnr[i, rows, :].astype(F32)) * scale
            unit = xhat[i, rows, :]
            m1 = jnp.mean(g, axis=-1, keepdims=True)
            m2 = jnp.mean(g * unit, axis=-1, keepdims=True)
            inv = jnp.mean(rstd[i, rows, :], axis=-1, keepdims=True)
            xhat[i, rows, :] = inv * (g - m1 - unit * m2)

        rows = dot(tab[0:32, :], xhat[i], precision=lax.Precision.HIGHEST)
        gl_o[i] = rows[0:16]
        r["rim_s"][0, 4 * i : 4 * i + 4, :] = rows[16:20]
        r["rim_s"][1, 4 * i : 4 * i + 4, :] = rows[20:24]
        if i == 1:
            advance(4, 1)
            finish(2)
    rims = [
        c.send(r["rim_s"].at[0], r["rim_r"].at[0], r["rim_ss"].at[0], r["rim_rs"].at[0], me.shard(-1)),
        c.send(r["rim_s"].at[1], r["rim_r"].at[1], r["rim_ss"].at[1], r["rim_rs"].at[1], me.shard(1)),
    ]
    advance(5, 1)
    finish(3)
    loss_next(3)
    out_stage(0, 3)
    out_stage(1, 3)
    own_out = obuf.at[me.core]
    oc = c.send(own_out, own_out, r["oc_ss"], r["oc_rs"], me.core_peer())
    finish(4)
    arrive(rims)
    for i in range(4):
        gl_o[i, 12:16, :] += r["rim_r"][0, 4 * i : 4 * i + 4, :] * has_next
        gl_o[i, 0:4, :] += r["rim_r"][1, 4 * i : 4 * i + 4, :] * has_prev
    oc.wait_recv()
    for core in range(2):
        for b in range(56):
            vg, hg = b // 8, b % 8
            rows = min(16, VARS - 16 * vg)
            block = obuf[core, b // 16, (b // 4) % 4, b % 4].astype(F32) * (1.0 / SCALE)
            at = core * HALF + 256 * hg
            gwo_o[16 * vg : 16 * vg + rows, at : at + 256] = block[0:rows]
    finish(5)
    for k in range(6):
        arrive(finals[k])
    for xl in range(2):
        for core in range(2):
            gwi_o[16 * xl : 16 * xl + 16, HALF * core : HALF * core + HALF] = fin[xl, core]
    c.drain()


SCRATCH["small_g"] = pltpu.VMEM((16, 32, 128), F32)


def local(latent, edge_index, edge_weight, noise_seed, noise_table, w_in, w_out, target, area_weight):
    vmem = pl.BlockSpec(memory_space=pltpu.VMEM)
    smem = pl.BlockSpec(memory_space=pltpu.SMEM)
    loss, grad_latent, grad_in, grad_out = pl.pallas_call(
        kernel,
        out_shape=(
            jax.ShapeDtypeStruct((8, 128), F32),
            jax.ShapeDtypeStruct((4, 16, LAT), F32),
            jax.ShapeDtypeStruct((32, 2 * HALF), F32),
            jax.ShapeDtypeStruct((VARS, 2 * HALF), F32),
        ),
        in_specs=[vmem, vmem, vmem, smem] + [vmem] * 5,
        out_specs=(vmem,) * 4,
        scratch_shapes=list(SCRATCH.values()),
        compiler_params=pltpu.CompilerParams(
            collective_id=0, has_side_effects=True, vmem_limit_bytes=63 * 2**20
        ),
    )(latent, edge_index, edge_weight, noise_seed, noise_table, w_in, w_out, target, area_weight.reshape(1, -1))
    return (jnp.sum(loss) / POINTS, grad_latent, grad_in, grad_out)


def solution(mesh):
    return jax.shard_map(
        local,
        mesh=mesh,
        in_specs=(
            P("member", "space", None),
            P(None, "space"),
            P(None, "space"),
            P("member"),
            P(),
            P("space", None),
            P(),
            P(None, "space"),
            P("space"),
        ),
        out_specs=(P(), P("member", "space", None), P("space", None), P()),
        check_vma=False,
    )
```

time: 1030 us -> 126 us (0.12)
  waiting for transfers between devices: 848 us -> 0 us
  Pallas kernels: 0 us -> 116 us
  blocking collectives: 87.7 us -> 0 us
  matrix products: 49.1 us -> 0 us
  between operations: 16.3 us -> 2.43 us
  starting transfers between devices: 12 us -> 0 us
    reduce_scatter x1 -> x0, waiting for transfers between devices: 704 us -> none  [local(): lax.psum_scatter(reordered, ('member', 'space'), scatter_dimension=0, til...]
    pallas_call x0 -> x1, Pallas kernels: none -> 116 us  [local(): pl.pallas_call(kernel, out_shape=(jax.ShapeDtypeStruct((8, 128), F32), ja...]
    all_gather x1 -> x0, waiting for transfers between devices: 90.9 us -> none  [local(): w_whole = lax.all_gather(w_in, 'space', axis=0, tiled=True)]
    psum x1 -> x0, blocking collectives: 65.3 us -> none  [local(): lax.psum((local_loss, grad_out_part), ('member', 'space'))]
    dot_general x9 -> x0, matrix products: 49.1 us -> none  [the longest x1 13 us: local(): jnp.einsum('mpd,dh->mph', normed, w_whole, preferred_element_type=jnp.flo...]
    psum x1 -> x0, waiting for transfers between devices: 46.6 us -> none  [local(): lax.psum((local_loss, grad_out_part), ('member', 'space'))]
    all_gather x2 -> x0, blocking collectives: 22.4 us -> none  [the longest x1 13.1 us: local(): grad_in = lax.all_gather(own_piece, 'member', axis=0, tiled=True)]
    ppermute x4 -> x0, starting transfers between devices: 11.6 us -> none  [the longest x2 9.03 us: padded(): before = lax.ppermute(last, axis, up)]
  transfers between devices with their start and end apart: 7 -> 0, of which waited for: 5 -> 0; matrix products, arithmetic and copies ran while one was open for 4% -> 0% of each run, Pallas kernels for 0% -> 0%
where the time goes in v1:
time: 126 us
  Pallas kernels  116 us (92%)
  local copies, waits for them, and re-layouts  6.3 us (5%)
  between operations  2.43 us (2%)
  other arithmetic  1.29 us (1%)
    pallas_call x1, Pallas kernels, local(): pl.pallas_call(kernel, out_shape=(jax.ShapeDtypeStruct((8, 128), F32), ja...  116 us
    unnamed x3, local copies, waits for them, and re-layouts  6.3 us

profile of v1, /device:TPU:1, one launch (start us, length us, event | category | flops | bytes accessed | tf_op | source)
XLA Modules:
  0.0 125.6 jit_solution(17171530479034630366)
XLA Ops:
  0.6 115.6 %shard_map.120 = (f32[8,128]{1,0:T(8,128)}, f32[4,16,1024]{2,1,0:T(8,128)}, f32[32,4096]{1,0:T(8,128)}, f32[100,4096]{1,0:T(8,128)}) custom-call(bf16[4,16,1024]{2,1,0:T(8,128)(2,1)} %lat.1, s32[3,128]{1,0:T(4,128)} %eidx.1, f32[3,128]{1,0:T(4,128)} %ewt.1, s32[4]{0:T(128)} %seed.1, f32[64,1024]{1,0:T(8,128)} %ntab.1, bf16[32,4096]{1,0:T(8,128)(2,1)} %w_in.1, ...), custom_call_target="tpu_custom_call" | custom-call | tf_op jit(solution)/shard_map/pallas_call | solution.py:590
  116.3 1.3 %reduce_sum.9 = f32[]{:T(128)} reduce(f32[8,128]{1,0:T(8,128)} %get-tuple-element.8, f32[]{:T(128)} %constant.1.clone.1), dimensions={0,1}, to_apply=%region_0.0 | reduce | flops 1023 | bytes 4104 | tf_op jit(solution)/shard_map/reduce_sum | solution.py:605
  118.2 1.7 %copy.16 = f32[4,16,1024]{2,1,0:T(8,128)} copy(f32[4,16,1024]{2,1,0:T(8,128)} %get-tuple-element.17) | data formatting | bytes 524288
  119.9 1.9 %copy.17 = f32[32,4096]{1,0:T(8,128)} copy(f32[32,4096]{1,0:T(8,128)} %get-tuple-element.18) | data formatting | bytes 1048576
  121.7 2.8 %copy.18 = f32[100,4096]{1,0:T(8,128)} copy(f32[100,4096]{1,0:T(8,128)} %get-tuple-element.19) | data formatting | bytes 3276800

commit v2 on v1

v2 whole, which is shorter than its diff:
```python
import jax
import jax.numpy as jnp
from jax import lax
from jax.experimental import pallas as pl
from jax.experimental.pallas import tpu as pltpu
from jax.sharding import PartitionSpec as P

VARS = 100
HALO = 4
MEMBERS = 16
POINTS = 4096
F32 = jnp.float32
BF16 = jnp.bfloat16
EPS = 1e-05
SMOOTH = 0.04
SCALE = 1024.0
PAIR = 1.0 / (MEMBERS * (MEMBERS - 1))
GELU_C = 0.7978845608028654
MESH = pl.DeviceIdType.MESH

LAT = 1024
HALF = 2048
WIDE = HALF + 256
GROUPS = [
    ("yzx", 0, 384),
    ("zyx", 384, 384),
    ("xzy", 768, 384),
    ("zxy", 1152, 384),
    ("xyz", 1536, 256),
    ("yxz", 1792, 256),
]
SEND_ORDER = (0, 2, 4, 1, 3, 5)
CHUNKS = [(0, (0,)), (768, (2,)), (1536, (4,)), (256, (0, 1)), (512, (1,)), (1024, (2, 3)), (1280, (3,)), (1792, (5,))]
PARTS = [(0, 256), (256, 256), (1536, 512), (512, 512), (1024, 512), (2048, 256)]
ORDERS = ["xyz", "yzx", "zyx", "xzy", "yxz", "zxy"]
X1, Y1, Z2, X2, Y2, OUT = range(6)

DMA = pltpu.SemaphoreType.DMA
SCRATCH = dict(
    wbuf=pltpu.VMEM((4, 4, 4, 16, HALF), BF16),
    wo=pltpu.VMEM((128, HALF), BF16),
    wo_t=pltpu.VMEM((HALF, 128), BF16),
    nbuf=pltpu.VMEM((4, 8, 32, LAT), BF16),
    n_t=pltpu.VMEM((LAT, 1024), BF16),
    xhat=pltpu.VMEM((4, 128, LAT), F32),
    rstd=pltpu.VMEM((4, 128, 128), F32),
    tab=pltpu.VMEM((128, 128), F32),
    small=pltpu.VMEM((3, 128, 128), F32),
    hid=pltpu.VMEM((4, 256, HALF), BF16),
    big=pltpu.VMEM((4, 4, 4, 16, WIDE), F32),
    gpre=pltpu.VMEM((4, 256, HALF), BF16),
    halo_s=pltpu.VMEM((2, 16, LAT), BF16),
    halo_r=pltpu.VMEM((4, 16, LAT), BF16),
    fpart=pltpu.VMEM((4, 8, 32, 128), F32),
    fcore=pltpu.VMEM((2, 8, 32, 128), F32),
    fsum=pltpu.VMEM((2, 8, 32, 128), F32),
    fother=pltpu.VMEM((8, 32, 128), F32),
    gf=pltpu.VMEM((4, 8, 32, 128), BF16),
    gfo=pltpu.VMEM((8, 32, 128), BF16),
    gf_t=pltpu.VMEM((128, 1024), BF16),
    sb1=pltpu.VMEM((4, 4, 4, 16, WIDE), BF16),
    rb1=pltpu.VMEM((3, 4, 4, 16, WIDE), BF16),
    q1=pltpu.VMEM((4, 4, 16, WIDE), F32),
    sb2=pltpu.VMEM((4, 4, 16, WIDE), BF16),
    rb2=pltpu.VMEM((3, 4, 16, WIDE), BF16),
    q2=pltpu.VMEM((4, 16, WIDE), F32),
    sb3=pltpu.VMEM((4, 16, WIDE), BF16),
    rb3=pltpu.VMEM((3, 16, WIDE), BF16),
    fin=pltpu.VMEM((2, 2, 16, HALF), F32),
    obuf=pltpu.VMEM((2, 4, 4, 4, 16, 256), BF16),
    gno=pltpu.VMEM((4, 4, 32, LAT), F32),
    gns=pltpu.VMEM((4, 4, 32, LAT), BF16),
    gnr=pltpu.VMEM((4, 4, 32, LAT), BF16),
    rim_s=pltpu.VMEM((2, 16, LAT), F32),
    rim_r=pltpu.VMEM((4, 16, LAT), F32),
    gwo=pltpu.VMEM((VARS, 2 * HALF), F32),
    glat=pltpu.VMEM((4, 16, LAT), F32),
    out_sem=DMA((6,)),
    loss_s=pltpu.VMEM((4, 8, 128), F32),
    loss_r=pltpu.VMEM((10, 8, 128), F32),
    ag_ss=DMA((18, 3)),
    ag_rs=DMA((18, 3)),
    rs_ss=DMA((6, 3, 3)),
    rs_rs=DMA((6, 3, 3)),
    oa_ss=DMA((2, 3, 3)),
    oa_rs=DMA((2, 3, 3)),
    fin_ss=DMA((5, 3)),
    fin_rs=DMA((5, 3)),
    n_ss=DMA((4,)),
    n_rs=DMA((4,)),
    gn_ss=DMA((4,)),
    gn_rs=DMA((4,)),
    halo_ss=DMA((3,)),
    halo_rs=DMA((3,)),
    rim_ss=DMA((4,)),
    rim_rs=DMA((4,)),
    f_ss=DMA((2,)),
    f_rs=DMA((2,)),
    g_ss=DMA((3,)),
    g_rs=DMA((3,)),
    oc_ss=DMA,
    oc_rs=DMA,
    l_ss=DMA((10,)),
    l_rs=DMA((10,)),
)


def dot(a, b, dims=((1,), (0,)), precision=None):
    return lax.dot_general(a, b, (dims, ((), ())), precision=precision, preferred_element_type=F32)


class Place:
    def __init__(self):
        m, s = lax.axis_index("member"), lax.axis_index("space")
        self.m, self.s = m, s
        self.xl, self.core = m // 2, m % 2
        self.y, self.z, self.xh = s // 8, (s // 2) % 4, s % 2
        self.x = self.xh * 2 + self.xl
        self.turn = 1 - 2 * self.xh

    def device(self, y, z, x):
        return ((x % 2) * 2 + self.core, (y * 4 + z) * 2 + x // 2)

    def at(self, axis):
        return getattr(self, axis)

    def peer(self, axis, step):
        q = dict(y=self.y, z=self.z, x=self.x)
        q[axis] = (q[axis] + step) % 4
        return self.device(**q)

    def core_peer(self):
        return (self.xl * 2 + 1 - self.core, self.s)

    def pair_peer(self):
        return ((1 - self.xl) * 2 + self.core, self.s)

    def cross_peer(self):
        return ((1 - self.xl) * 2 + 1 - self.core, self.s)


class Copies:
    def __init__(self):
        self.sent = []

    def send(self, src, dst, ss, rs, device):
        copy = pltpu.make_async_remote_copy(
            src_ref=src, dst_ref=dst, send_sem=ss, recv_sem=rs, device_id=device, device_id_type=MESH
        )
        copy.start()
        self.sent.append(copy)
        return copy

    def drain(self):
        for copy in self.sent:
            copy.wait_send()


def arrive(copies):
    for copy in copies:
        copy.wait_recv()


def kernel(lat, eidx, ewt, seed, ntab, w_in, w_out, target, area, loss_o, gl_o, gwi_o, gwo_o, *refs):
    r = dict(zip(SCRATCH, refs))
    wbuf, big, nbuf, n_t, hid, gpre, wo = (r[k] for k in ("wbuf", "big", "nbuf", "n_t", "hid", "gpre", "wo"))
    xhat, rstd, tab, small = r["xhat"], r["rstd"], r["tab"], r["small"]
    me = Place()
    c = Copies()
    col0 = pl.multiple_of(me.core * HALF, 128)

    friends = [me.peer(a, k) for a in "yzx" for k in (1, 2, 3)]
    friends += [me.core_peer(), me.cross_peer()]
    barrier = pltpu.get_barrier_semaphore()
    for d in friends:
        pl.semaphore_signal(barrier, inc=1, device_id=d, device_id_type=MESH)

    wbuf[me.y, me.z, me.x] = w_in[pl.ds(pl.multiple_of(me.xl * 16, 16), 16), pl.ds(col0, HALF)]
    lat32 = [lat[i].astype(F32) for i in range(4)]
    r["halo_s"][0] = jnp.concatenate([v[12:16] for v in lat32], axis=0).astype(BF16)
    r["halo_s"][1] = jnp.concatenate([v[0:4] for v in lat32], axis=0).astype(BF16)
    pl.semaphore_wait(barrier, len(friends))

    halo_s, halo_r = r["halo_s"], r["halo_r"]

    def halo_send(src, dst, k, device):
        return c.send(src, dst, r["halo_ss"].at[k], r["halo_rs"].at[k], device)

    halo = [halo_send(halo_s, halo_r.at[pl.ds(0, 2)], 0, me.peer("x", 2))]

    def gather_send(slot, group, stage, c0, cw):
        order = GROUPS[group][0]
        index = tuple(pl.ds(0, 4) if a in order[:stage] else pl.ds(me.at(a), 1) for a in "yzx")
        index += (slice(None), pl.ds(c0, cw))
        here = wbuf.at[index]
        return [
            c.send(here, here, r["ag_ss"].at[slot, i - 1], r["ag_rs"].at[slot, i - 1], me.peer(order[stage], i))
            for i in (2, 1, 3)
        ]

    gathered = {}

    def gather_stage(stage):
        for g in SEND_ORDER:
            _, c0, cw = GROUPS[g]
            arrive(gathered.pop(g, []))
            gathered[g] = gather_send(6 * stage + g, g, stage, c0, cw)

    gather_stage(0)

    node = lax.broadcasted_iota(jnp.int32, (128, 128), 0)
    row_of = jnp.where(node < 16, node + HALO, jnp.where(node < 20, node - 16, jnp.where(node < 24, node, -1)))
    table_t = jnp.zeros((128, 128), F32)
    for k in range(3):
        table_t = table_t + jnp.where(row_of == eidx[k : k + 1, :], ewt[k : k + 1, :], 0.0)
    tab[...] = table_t
    table = table_t.T[:, :32]
    t_hi = table.astype(BF16)
    t_rest = table - t_hi.astype(F32)
    t_mid = t_rest.astype(BF16)
    t_low = (t_rest - t_mid.astype(F32)).astype(BF16)
    small[0] = jnp.zeros((128, 128), F32)
    small[0, 0:VARS] = target[...]
    small[1] = small[0].T
    small[2] = jnp.broadcast_to(area[...], (128, 128)).T

    arrive(halo)
    halo = [halo_send(halo_r.at[me.xh], halo_r.at[2], 1, me.peer("z", me.turn))]
    gather_stage(1)
    arrive(halo)
    halo = [halo_send(halo_r.at[2], halo_r.at[3], 2, me.peer("y", me.turn))]
    big[0, 0:2, :, :, 0:HALF] = jnp.zeros((2, 4, 16, HALF), F32)
    head = w_out[:, pl.ds(col0, HALF)].astype(F32)
    for v in range(6):
        big[0, v // 4, v % 4, :, 0:HALF] = head[16 * v : 16 * v + 16]
    big[0, 1, 2, 0:4, 0:HALF] = head[96:100]
    wo[...] = big[0, 0:2, :, :, 0:HALF].reshape(128, HALF).astype(BF16)
    r["wo_t"][...] = wo[...].T

    gather_stage(2)

    arrive(halo)
    has_prev = (me.s > 0).astype(F32)
    has_next = (me.s < 31).astype(F32)
    prev_at = jnp.where(me.xh == 0, jnp.where(me.z == 0, 3, 2), 0)
    next_at = jnp.where(me.xh == 1, jnp.where(me.z == 3, 3, 2), 1)
    prev_rows = halo_r[prev_at].astype(F32) * has_prev
    next_rows = halo_r[next_at].astype(F32) * has_next
    normed = []
    for i in range(4):
        edges = [lat[i].astype(F32), prev_rows[4 * i : 4 * i + 4], next_rows[4 * i : 4 * i + 4]]
        window = jnp.concatenate(edges + [jnp.zeros((8, LAT), F32)], axis=0).astype(BF16)
        xhat[i] = dot(t_hi, window) + dot(t_mid, window) + dot(t_low, window)
        scale = 1.0 + ntab[pl.ds(seed[i], 1), :]
        row = me.core * 4 + i

        @pl.loop(0, 4)
        def _(j):
            rows = pl.ds(pl.multiple_of(j * 32, 32), 32)
            a = xhat[i, rows, :]
            centred = a - jnp.mean(a, axis=-1, keepdims=True)
            inv = lax.rsqrt(jnp.mean(centred * centred, axis=-1, keepdims=True) + EPS)
            unit = centred * inv
            xhat[i, rows, :] = unit
            rstd[i, rows, :] = jnp.broadcast_to(inv, (32, 128))
            nbuf[j, row] = (unit * scale).astype(BF16)

        normed.append(c.send(nbuf.at[:, row], nbuf.at[:, row], r["n_ss"].at[i], r["n_rs"].at[i], me.core_peer()))
    arrive(normed)
    for g in range(4):
        n_t[:, 256 * g : 256 * g + 256] = nbuf[g].reshape(256, LAT).T

    fpart, fcore, fsum, fother, gf, gfo = (r[k] for k in ("fpart", "fcore", "fsum", "fother", "gf", "gfo"))
    fpart[...] = jnp.zeros_like(fpart)
    for c0, sources in CHUNKS:
        for g in sources:
            arrive(gathered.pop(g, []))
        cols = slice(c0, c0 + 256)

        w = wbuf[:, :, :, :, cols].reshape(LAT, 256)
        for h in range(4):
            pre = dot(nbuf[h].reshape(256, LAT), w)
            sq = pre * pre
            t = jnp.tanh(pre * (GELU_C + (GELU_C * 0.044715) * sq))
            cdf = 0.5 + 0.5 * t
            act = (pre * cdf).astype(BF16)
            hid[h, :, cols] = act
            slope = cdf + (0.5 * pre) * (1.0 - t * t) * (GELU_C + (3.0 * GELU_C * 0.044715) * sq)
            big[h, :, :, :, cols] = slope.reshape(4, 4, 16, 256)
        for h in range(4):
            fpart[h] += dot(hid[h, :, cols], r["wo_t"][cols, :]).reshape(8, 32, 128)

    f1 = c.send(
        fpart.at[pl.ds(2 * (1 - me.core), 2)], fcore, r["f_ss"].at[0], r["f_rs"].at[0], me.core_peer()
    )
    f1.wait_recv()
    for g in range(2):
        fsum[g] = fpart[2 * me.core + g] + fcore[g]
    f2 = c.send(fsum.at[1 - me.xl], fother, r["f_ss"].at[1], r["f_rs"].at[1], me.pair_peer())
    group = me.core * 2 + me.xl
    f2.wait_recv()

    r["loss_s"][0] = jnp.zeros((8, 128), F32)
    lane = lax.broadcasted_iota(jnp.int32, (8, 128), 1)

    @pl.loop(0, 4)
    def _(j):
        rows = pl.ds(pl.multiple_of(j * 8, 8), 8)
        point = pl.ds(pl.multiple_of(group * 32 + j * 8, 8), 8)
        f = [fsum[me.xl, i, rows, :] for i in range(8)] + [fother[i, rows, :] for i in range(8)]
        weighted = jnp.where(lane < VARS, small[2, point, :] / VARS, 0.0)
        goal = small[1, point, :]
        signs = [jnp.zeros((8, 128), F32) for _ in range(MEMBERS)]
        pairs = jnp.zeros((8, 128), F32)
        for a in range(MEMBERS):
            for b in range(a + 1, MEMBERS):
                d = f[a] - f[b]
                q = d * d + SMOOTH
                inv = lax.rsqrt(q)
                pairs = pairs + q * inv
                sl = d * inv
                signs[a] = signs[a] + sl
                signs[b] = signs[b] - sl
        misfits = jnp.zeros((8, 128), F32)
        for a in range(MEMBERS):
            d = f[a] - goal
            q = d * d + SMOOTH
            inv = lax.rsqrt(q)
            misfits = misfits + q * inv
            grad = (SCALE * weighted) * ((d * inv) * (1.0 / MEMBERS) - PAIR * signs[a])
            r["small_g"][a, rows, :] = grad
        term = misfits * (1.0 / MEMBERS) - PAIR * (pairs + MEMBERS * 0.5 * 0.2)
        r["loss_s"][0] += weighted * term

    for a in range(8):
        gf[group, a] = r["small_g"][a].astype(BF16)
        gfo[a] = r["small_g"][8 + a].astype(BF16)
    gs = [
        c.send(gfo, gf.at[group], r["g_ss"].at[0], r["g_rs"].at[0], me.pair_peer()),
        c.send(gf.at[group], gf.at[group], r["g_ss"].at[1], r["g_rs"].at[1], me.core_peer()),
    ]

    loss_s, loss_r = r["loss_s"], r["loss_r"]
    loss_pending = []

    def loss_send(level):
        if level == 0:
            loss_pending.append(
                [c.send(loss_s.at[0], loss_r.at[0], r["l_ss"].at[0], r["l_rs"].at[0], me.core_peer())]
            )
            return
        axis = "yzx"[level - 1]
        loss_pending.append(
            [
                c.send(
                    loss_s.at[level], loss_r.at[3 * level - 3 + i], r["l_ss"].at[3 * level - 3 + i],
                    r["l_rs"].at[3 * level - 3 + i], me.peer(axis, i),
                )
                for i in (1, 2, 3)
            ]
        )

    def loss_next(level):
        arrive(loss_pending[level])
        if level == 0:
            loss_s[1] = loss_s[0] + loss_r[0]
            return
        v = me.at("yzx"[level - 1])
        base = 3 * level - 3
        own, one, two, three = loss_s[level], loss_r[base + 1], loss_r[base + 2], loss_r[base + 3]
        total = (own + two) + (one + three)
        if level < 3:
            loss_s[level + 1] = total
        else:
            loss_o[...] = total

    loss_send(0)

    def back(h):
        @pl.loop(0, 2)
        def _(j):
            for k in range(4):
                cols = pl.ds(pl.multiple_of(j * 1024 + k * 256, 256), 256)
                slope = big[h, :, :, :, cols].reshape(256, 256)
                gpre[h, :, cols] = (dot(gf[h].reshape(256, 128), wo[:, cols]) * slope).astype(BF16)

    back(group)
    gs[1].wait_recv()
    back((1 - me.core) * 2 + me.xl)
    pair = me.core * 2 + 1 - me.xl
    gs[0].wait_recv()
    gs.append(c.send(gf.at[pair], gf.at[pair], r["g_ss"].at[2], r["g_rs"].at[2], me.core_peer()))
    back(pair)
    gs[2].wait_recv()
    back((1 - me.core) * 2 + 1 - me.xl)
    r["gf_t"][...] = gf[...].reshape(1024, 128).T

    sb1, rb1, q1, sb2, rb2, q2, sb3, rb3, fin, obuf = (
        r[k] for k in ("sb1", "rb1", "q1", "sb2", "rb2", "q2", "sb3", "rb3", "fin", "obuf")
    )
    flight = {}

    def pick(axis, axes, value, cols):
        return tuple(value if a == axis else slice(None) for a in axes) + (slice(None), cols)

    def scatter_send(k, stage):
        c0, cw = PARTS[k]
        cols, order = pl.ds(c0, cw), ORDERS[k]
        axis = order[stage]
        axes = [a for a in "yzx" if a not in order[:stage]]
        src, dst = ((sb1, rb1), (sb2, rb2), (sb3, rb3))[stage]
        flight[k] = []
        for i in (2, 1, 3):
            there = (me.at(axis) + i) % 4
            flight[k].append(
                c.send(
                    src.at[pick(axis, axes, there, cols)],
                    dst.at[(i - 1,) + (slice(None),) * (3 - stage) + (cols,)],
                    r["rs_ss"].at[k, stage, i - 1], r["rs_rs"].at[k, stage, i - 1], me.peer(axis, i),
                )
            )

    def scatter_add(k, stage):
        c0, cw = PARTS[k]
        cols, order = slice(c0, c0 + cw), ORDERS[k]
        axis = order[stage]
        axes = [a for a in "yzx" if a not in order[:stage]]
        arrive(flight[k])
        own = (big, q1, q2)[stage]
        dst = (rb1, rb2, rb3)[stage]
        where = me.at(axis)
        if stage == 2:
            total = own[where, :, cols]
            for i in range(3):
                total = total + dst[i, :, cols].astype(F32)
            return total
        spot = axes.index(axis)
        keep, send = ((q1, sb2), (q2, sb3))[stage]
        for v in range(4):
            if stage == 0:
                index = [v, slice(None)]
                index.insert(spot, where)
                total = own[tuple(index) + (slice(None), cols)]
                for i in range(3):
                    total = total + dst[i, v, :, :, cols].astype(F32)
                keep[v, :, :, cols] = total
                send[v, :, :, cols] = total.astype(BF16)
            else:
                index = [v]
                index.insert(spot, where)
                total = own[tuple(index) + (slice(None), cols)]
                for i in range(3):
                    total = total + dst[i, v, :, cols].astype(F32)
                keep[v, :, cols] = total
                send[v, :, cols] = total.astype(BF16)

    def advance(k, stage):
        scatter_add(k, stage)
        scatter_send(k, stage + 1)

    finals = {}

    def final_send(k, i, xl, device):
        c0, cw = PARTS[k]
        here = fin.at[xl, me.core, :, pl.ds(c0, cw)]
        return c.send(here, here, r["fin_ss"].at[k, i], r["fin_rs"].at[k, i], device)

    def finish(k):
        c0, cw = PARTS[k]
        fin[me.xl, me.core, :, c0 : c0 + cw] = scatter_add(k, 2) * (1.0 / SCALE)
        finals[k] = [
            final_send(k, 0, me.xl, me.pair_peer()),
            final_send(k, 1, me.xl, me.core_peer()),
        ]

    def finish_pass(k):
        finals[k][0].wait_recv()
        finals[k][0] = final_send(k, 2, 1 - me.xl, me.core_peer())

    out_flight = {}

    def out_stage(part, stage):
        order = ("yzx", "xyz")[part]
        c0 = 128 * part
        if stage == 0:
            if part == 0:
                obuf[me.core, me.y, me.z, me.x] = scatter_add(OUT, 2).astype(BF16)
        else:
            arrive(out_flight[part])
        if stage == 3:
            return
        index = (me.core,)
        index += tuple(pl.ds(0, 4) if a in order[:stage] else pl.ds(me.at(a), 1) for a in "yzx")
        index += (slice(None), pl.ds(c0, 128))
        out_flight[part] = [
            c.send(
                obuf.at[index], obuf.at[index], r["oa_ss"].at[part, stage, i - 1], r["oa_rs"].at[part, stage, i - 1],
                me.peer(order[stage], i),
            )
            for i in (2, 1, 3)
        ]

    @pl.loop(0, 8)
    def _(hg):
        cols = pl.ds(pl.multiple_of(hg * 256, 256), 256)
        part = dot(r["gf_t"][...], hid[:, :, cols].reshape(1024, 256))
        for vg in range(8):
            block = part[16 * vg : 16 * vg + 16]
            y, z, x = vg // 2, (vg % 2) * 2 + hg // 4, hg % 4
            big[y, z, x, :, HALF:WIDE] = block
            sb1[y, z, x, :, HALF:WIDE] = block.astype(BF16)

    scatter_send(OUT, 0)

    def column_part(k):
        c0, cw = PARTS[k]
        for c1 in range(c0, c0 + cw, 256):
            cols = slice(c1, c1 + 256)
            for y in range(4):
                rows = slice(256 * y, 256 * y + 256)
                grad = dot(n_t[rows, :], gpre[:, :, cols].reshape(1024, 256)).reshape(4, 4, 16, 256)
                big[y, :, :, :, cols] = grad
                sb1[y, :, :, :, cols] = grad.astype(BF16)
        scatter_send(k, 0)

    gno, gns, gnr = r["gno"], r["gns"], r["gnr"]

    def grad_normed(core, dst):
        members = pl.ds(pl.multiple_of(core * 128, 128), 128)

        @pl.loop(0, 4)
        def _(n):
            lanes = pl.ds(pl.multiple_of(n * 256, 256), 256)
            part = dot(gpre[:, members, :].reshape(512, HALF), wbuf[n].reshape(256, HALF), ((1,), (1,)))
            dst[:, :, :, lanes] = part.reshape(4, 4, 32, 256).astype(dst.dtype)

    glat, rim_s, rim_r = r["glat"], r["rim_s"], r["rim_r"]

    def norm_back(i):
        scale = 1.0 + ntab[pl.ds(seed[i], 1), :]
        gn[i].wait_recv()
        for j in range(4):
            rows = slice(32 * j, 32 * j + 32)
            g = (gno[j, i] + gnr[j, i].astype(F32)) * scale
            unit = xhat[i, rows, :]
            m1 = jnp.mean(g, axis=-1, keepdims=True)
            m2 = jnp.mean(g * unit, axis=-1, keepdims=True)
            inv = rstd[i, rows, :][:, 0:1]
            xhat[i, rows, :] = inv * (g - m1 - unit * m2)
        rows = dot(tab[0:32, :], xhat[i], precision=lax.Precision.HIGHEST)
        glat[i] = rows[0:16]
        rim_s[0, 4 * i : 4 * i + 4, :] = rows[16:20]
        rim_s[1, 4 * i : 4 * i + 4, :] = rows[20:24]

    def rim_send(src, dst, k, device):
        return c.send(src, dst, r["rim_ss"].at[k], r["rim_rs"].at[k], device)

    for k in (X1, Y1, Z2, X2, Y2):
        column_part(k)
        if k == Y1:
            loss_next(0)
            loss_send(1)
    grad_normed(1 - me.core, gns)
    gn = [c.send(gns.at[:, i], gnr.at[:, i], r["gn_ss"].at[i], r["gn_rs"].at[i], me.core_peer()) for i in range(4)]
    for k in (OUT, X1, Y1):
        advance(k, 0)
    loss_next(1)
    loss_send(2)
    grad_normed(me.core, gno)
    norm_back(0)
    norm_back(1)
    for k in (OUT, X1, Y1):
        advance(k, 1)
    loss_next(2)
    loss_send(3)
    norm_back(2)
    norm_back(3)
    near = rim_send(rim_s.at[1 - me.xh], rim_r.at[0], 0, me.peer("x", 2))
    far = rim_send(rim_s.at[me.xh], rim_r.at[1], 1, me.peer("z", -me.turn))
    out_stage(0, 0)
    out_stage(1, 0)
    finish(X1)
    finish(Y1)
    for k in (Z2, X2, Y2):
        advance(k, 0)
    far.wait_recv()
    far = rim_send(rim_r.at[1], rim_r.at[2], 2, me.peer("y", -me.turn))
    out_stage(0, 1)
    out_stage(1, 1)
    for k in (Z2, X2, Y2):
        advance(k, 1)
    far.wait_recv()
    carried = jnp.where(me.xh == 0, me.z == 3, me.z == 0)
    last = rim_send(rim_r.at[jnp.where(carried, 2, 1)], rim_r.at[3], 3, me.peer("x", 2))
    out_stage(0, 2)
    out_stage(1, 2)
    for k in (Z2, X2, Y2):
        finish(k)
    for k in (X1, Y1):
        finish_pass(k)
    loss_next(3)
    out_stage(0, 3)
    out_stage(1, 3)
    own_out = obuf.at[me.core]
    oc = c.send(own_out, own_out, r["oc_ss"], r["oc_rs"], me.core_peer())
    near.wait_recv()
    last.wait_recv()
    from_next = rim_r[jnp.where(me.xh == 0, 0, 3)] * has_next
    from_prev = rim_r[jnp.where(me.xh == 0, 3, 0)] * has_prev
    for i in range(4):
        glat[i, 12:16, :] += from_next[4 * i : 4 * i + 4]
        glat[i, 0:4, :] += from_prev[4 * i : 4 * i + 4]
    leave = [pltpu.make_async_copy(glat, gl_o, r["out_sem"].at[0])]
    leave[0].start()
    for k in (Z2, X2, Y2):
        finish_pass(k)
    oc.wait_recv()
    gwo = r["gwo"]
    for core in range(2):
        for b in range(56):
            vg, hg = b // 8, b % 8
            rows = min(16, VARS - 16 * vg)
            block = obuf[core, b // 16, (b // 4) % 4, b % 4].astype(F32) * (1.0 / SCALE)
            at = core * HALF + 256 * hg
            gwo[16 * vg : 16 * vg + rows, at : at + 256] = block[0:rows]
    leave.append(pltpu.make_async_copy(gwo, gwo_o, r["out_sem"].at[1]))
    leave[1].start()
    for k in finals:
        arrive(finals[k])
    for xl in range(2):
        for core in range(2):
            dst = gwi_o.at[pl.ds(16 * xl, 16), pl.ds(HALF * core, HALF)]
            leave.append(pltpu.make_async_copy(fin.at[xl, core], dst, r["out_sem"].at[2 + 2 * xl + core]))
            leave[-1].start()
    for copy in leave:
        copy.wait()
    c.drain()


SCRATCH["small_g"] = pltpu.VMEM((16, 32, 128), F32)


def hand_on(loss, gl, gwi, gwo, loss_o, gl_o, gwi_o, gwo_o):
    loss_o[0, 0] = jnp.sum(loss[...]) * (1.0 / POINTS)
    gl_o[...] = gl[...]
    gwi_o[...] = gwi[...]
    gwo_o[...] = gwo[...]


def local(latent, edge_index, edge_weight, noise_seed, noise_table, w_in, w_out, target, area_weight):
    vmem = pl.BlockSpec(memory_space=pltpu.VMEM)
    smem = pl.BlockSpec(memory_space=pltpu.SMEM)
    anywhere = pl.BlockSpec(memory_space=pl.ANY)
    grads = (
        jax.ShapeDtypeStruct((4, 16, LAT), F32),
        jax.ShapeDtypeStruct((32, 2 * HALF), F32),
        jax.ShapeDtypeStruct((VARS, 2 * HALF), F32),
    )
    made = pl.pallas_call(
        kernel,
        out_shape=(jax.ShapeDtypeStruct((8, 128), F32),) + grads,
        in_specs=[vmem, vmem, vmem, smem] + [vmem] * 5,
        out_specs=(vmem,) + (anywhere,) * 3,
        scratch_shapes=list(SCRATCH.values()),
        compiler_params=pltpu.CompilerParams(
            collective_id=0, has_side_effects=True, vmem_limit_bytes=63 * 2**20
        ),
    )(latent, edge_index, edge_weight, noise_seed, noise_table, w_in, w_out, target, area_weight.reshape(1, -1))
    loss, grad_latent, grad_in, grad_out = pl.pallas_call(
        hand_on,
        out_shape=(jax.ShapeDtypeStruct((1, 1), F32),) + grads,
        in_specs=[vmem] * 4,
        out_specs=(smem,) + (vmem,) * 3,
    )(*made)
    return (loss[0, 0], grad_latent, grad_in, grad_out)


def solution(mesh):
    return jax.shard_map(
        local,
        mesh=mesh,
        in_specs=(
            P("member", "space", None),
            P(None, "space"),
            P(None, "space"),
            P("member"),
            P(),
            P("space", None),
            P(),
            P(None, "space"),
            P("space"),
        ),
        out_specs=(P(), P("member", "space", None), P("space", None), P()),
        check_vma=False,
    )
```

time: 126 us -> 106 us (0.84)
  Pallas kernels: 116 us -> 105 us
  local copies, waits for them, and re-layouts: 6.3 us -> 0 us
  between operations: 2.43 us -> 0.8 us
  other arithmetic: 1.29 us -> 0 us
    pallas_call x1 -> x2, Pallas kernels: 116 us -> 105 us  [the longest x1 102 us: local(): pl.pallas_call(kernel, out_shape=(jax.ShapeDtypeStruct((8, 128), F32),) +...]
    unnamed x3 -> x0, local copies, waits for them, and re-layouts: 6.3 us -> none
    reduce_sum x1 -> x0, other arithmetic: 1.29 us -> none  [local(): return (jnp.sum(loss) / POINTS, grad_latent, grad_in, grad_out)]
where the time goes in v2:
time: 106 us
  Pallas kernels  105 us (99%)
    pallas_call x1, Pallas kernels, local(): pl.pallas_call(kernel, out_shape=(jax.ShapeDtypeStruct((8, 128), F32),) +...  102 us
    pallas_call x1, Pallas kernels, local(): pl.pallas_call(hand_on, out_shape=(jax.ShapeDtypeStruct((1, 1), F32),) +...  3.2 us

profile of v2, /device:TPU:1, one launch (start us, length us, event | category | flops | bytes accessed | tf_op | source)
XLA Modules:
  0.0 106.0 jit_solution(7498962301633690208)
XLA Ops:
  0.6 102.0 %shard_map.120 = (f32[8,128]{1,0:T(8,128)}, f32[4,16,1024]{2,1,0:T(8,128)}, f32[32,4096]{1,0:T(8,128)}, f32[100,4096]{1,0:T(8,128)}) custom-call(bf16[4,16,1024]{2,1,0:T(8,128)(2,1)} %lat.1, s32[3,128]{1,0:T(4,128)} %eidx.1, f32[3,128]{1,0:T(4,128)} %ewt.1, s32[4]{0:T(128)} %seed.1, f32[64,1024]{1,0:T(8,128)} %ntab.1, bf16[32,4096]{1,0:T(8,128)(2,1)} %w_in.1, ...), custom_call_target="tpu_custom_call" | custom-call | tf_op jit(solution)/shard_map/pallas_call | solution.py:659
  102.7 3.2 %shard_map.121 = (f32[1,1]{1,0:T(1,128)}, f32[4,16,1024]{2,1,0:T(8,128)}, f32[32,4096]{1,0:T(8,128)}, f32[100,4096]{1,0:T(8,128)}) custom-call(f32[8,128]{1,0:T(8,128)} %get-tuple-element.12.loss, f32[4,16,1024]{2,1,0:T(8,128)} %get-tuple-element.13.gl, f32[32,4096]{1,0:T(8,128)} %get-tuple-element.14.gwi, f32[100,4096]{1,0:T(8,128)} %get-tuple-element.15.gwo), custom_call_target="tpu_custom_call" | custom-call | tf_op jit(solution)/shard_map/pallas_call | solution.py:669

commit v3 on v2

--- a/solution.py
+++ b/solution.py
@@ -59,7 +59,8 @@
     gfo=pltpu.VMEM((8, 32, 128), BF16),
     gf_t=pltpu.VMEM((128, 1024), BF16),
     sb1=pltpu.VMEM((4, 4, 4, 16, WIDE), BF16),
-    rb1=pltpu.VMEM((3, 4, 4, 16, WIDE), BF16),
+    rb1=pltpu.VMEM((2, 4, 4, 16, WIDE), BF16),
+    relay=pltpu.VMEM((4, 4, 16, WIDE), BF16),
     q1=pltpu.VMEM((4, 4, 16, WIDE), F32),
     sb2=pltpu.VMEM((4, 4, 16, WIDE), BF16),
     rb2=pltpu.VMEM((3, 4, 16, WIDE), BF16),
@@ -82,6 +83,8 @@
     ag_rs=DMA((18, 3)),
     rs_ss=DMA((6, 3, 3)),
     rs_rs=DMA((6, 3, 3)),
+    ring_ss=DMA((9, 4)),
+    ring_rs=DMA((9, 4)),
     oa_ss=DMA((2, 3, 3)),
     oa_rs=DMA((2, 3, 3)),
     fin_ss=DMA((5, 3)),
@@ -403,16 +406,55 @@
     def pick(axis, axes, value, cols):
         return tuple(value if a == axis else slice(None) for a in axes) + (slice(None), cols)
 
+    relay = r["relay"]
+
+    def ring_start(k, c0):
+        axis = ORDERS[k][0]
+        opposite = (me.at(axis) + 2) % 4
+        slot = c0 // 256
+        flight[c0] = []
+        for i in range(2):
+            cols = pl.ds(c0 + 128 * i, 128)
+            flight[c0].append(
+                c.send(
+                    sb1.at[pick(axis, "yzx", opposite, cols)], relay.at[:, :, :, cols],
+                    r["ring_ss"].at[slot, i], r["ring_rs"].at[slot, i], me.peer(axis, 1 + 2 * i),
+                )
+            )
+
+    def ring_pass(k, c0):
+        axis = ORDERS[k][0]
+        spot = "yzx".index(axis)
+        slot = c0 // 256
+        passed = []
+        for i in range(2):
+            flight[c0][i].wait_recv()
+            there = (me.at(axis) + 1 + 2 * i) % 4
+            cols = slice(c0 + 128 * i, c0 + 128 * i + 128)
+            for v in range(4):
+                index = [v, slice(None)]
+                index.insert(spot, there)
+                index = tuple(index) + (slice(None), cols)
+                sb1[index] = (big[index] + relay[v, :, :, cols].astype(F32)).astype(BF16)
+            whole = pl.ds(c0, 256)
+            passed.append(
+                c.send(
+                    sb1.at[pick(axis, "yzx", there, whole)], rb1.at[i, :, :, :, whole],
+                    r["ring_ss"].at[slot, 2 + i], r["ring_rs"].at[slot, 2 + i], me.peer(axis, 1 + 2 * i),
+                )
+            )
+        flight[(k, 0)] = flight.get((k, 0), []) + passed
+
     def scatter_send(k, stage):
         c0, cw = PARTS[k]
         cols, order = pl.ds(c0, cw), ORDERS[k]
         axis = order[stage]
         axes = [a for a in "yzx" if a not in order[:stage]]
-        src, dst = ((sb1, rb1), (sb2, rb2), (sb3, rb3))[stage]
-        flight[k] = []
+        src, dst = ((sb2, rb2), (sb3, rb3))[stage - 1]
+        flight[(k, stage)] = []
         for i in (2, 1, 3):
             there = (me.at(axis) + i) % 4
-            flight[k].append(
+            flight[(k, stage)].append(
                 c.send(
                     src.at[pick(axis, axes, there, cols)],
                     dst.at[(i - 1,) + (slice(None),) * (3 - stage) + (cols,)],
@@ -425,7 +467,7 @@
         cols, order = slice(c0, c0 + cw), ORDERS[k]
         axis = order[stage]
         axes = [a for a in "yzx" if a not in order[:stage]]
-        arrive(flight[k])
+        arrive(flight[(k, stage)])
         own = (big, q1, q2)[stage]
         dst = (rb1, rb2, rb3)[stage]
         where = me.at(axis)
@@ -437,22 +479,14 @@
         spot = axes.index(axis)
         keep, send = ((q1, sb2), (q2, sb3))[stage]
         for v in range(4):
-            if stage == 0:
-                index = [v, slice(None)]
-                index.insert(spot, where)
-                total = own[tuple(index) + (slice(None), cols)]
-                for i in range(3):
-                    total = total + dst[i, v, :, :, cols].astype(F32)
-                keep[v, :, :, cols] = total
-                send[v, :, :, cols] = total.astype(BF16)
-            else:
-                index = [v]
-                index.insert(spot, where)
-                total = own[tuple(index) + (slice(None), cols)]
-                for i in range(3):
-                    total = total + dst[i, v, :, cols].astype(F32)
-                keep[v, :, cols] = total
-                send[v, :, cols] = total.astype(BF16)
+            index = [v] + [slice(None)] * (1 - stage)
+            index.insert(spot, where)
+            total = own[tuple(index) + (slice(None), cols)]
+            for i in range(2 + stage):
+                total = total + dst[(i, v) + (slice(None),) * (2 - stage) + (cols,)].astype(F32)
+            at = (v,) + (slice(None),) * (2 - stage) + (cols,)
+            keep[at] = total
+            send[at] = total.astype(BF16)
 
     def advance(k, stage):
         scatter_add(k, stage)
@@ -510,29 +544,23 @@
             big[y, z, x, :, HALF:WIDE] = block
             sb1[y, z, x, :, HALF:WIDE] = block.astype(BF16)
 
-    scatter_send(OUT, 0)
-
-    def column_part(k):
-        c0, cw = PARTS[k]
-        for c1 in range(c0, c0 + cw, 256):
-            cols = slice(c1, c1 + 256)
-            for y in range(4):
-                rows = slice(256 * y, 256 * y + 256)
-                grad = dot(n_t[rows, :], gpre[:, :, cols].reshape(1024, 256)).reshape(4, 4, 16, 256)
-                big[y, :, :, :, cols] = grad
-                sb1[y, :, :, :, cols] = grad.astype(BF16)
-        scatter_send(k, 0)
+    ring_start(OUT, HALF)
+
+    def column_part(k, c0):
+        cols = slice(c0, c0 + 256)
+        for y in range(4):
+            rows = slice(256 * y, 256 * y + 256)
+            grad = dot(n_t[rows, :], gpre[:, :, cols].reshape(1024, 256)).reshape(4, 4, 16, 256)
+            big[y, :, :, :, cols] = grad
+            sb1[y, :, :, :, cols] = grad.astype(BF16)
+        ring_start(k, c0)
 
     gno, gns, gnr = r["gno"], r["gns"], r["gnr"]
 
-    def grad_normed(core, dst):
+    def grad_normed(core, dst, n):
         members = pl.ds(pl.multiple_of(core * 128, 128), 128)
-
-        @pl.loop(0, 4)
-        def _(n):
-            lanes = pl.ds(pl.multiple_of(n * 256, 256), 256)
-            part = dot(gpre[:, members, :].reshape(512, HALF), wbuf[n].reshape(256, HALF), ((1,), (1,)))
-            dst[:, :, :, lanes] = part.reshape(4, 4, 32, 256).astype(dst.dtype)
+        part = dot(gpre[:, members, :].reshape(512, HALF), wbuf[n].reshape(256, HALF), ((1,), (1,)))
+        dst[:, :, :, 256 * n : 256 * n + 256] = part.reshape(4, 4, 32, 256).astype(dst.dtype)
 
     glat, rim_s, rim_r = r["glat"], r["rim_s"], r["rim_r"]
 
@@ -555,49 +583,69 @@
     def rim_send(src, dst, k, device):
         return c.send(src, dst, r["rim_ss"].at[k], r["rim_rs"].at[k], device)
 
-    for k in (X1, Y1, Z2, X2, Y2):
-        column_part(k)
-        if k == Y1:
-            loss_next(0)
-            loss_send(1)
-    grad_normed(1 - me.core, gns)
+    column_part(X1, 0)
+    column_part(Y1, 256)
+    column_part(Z2, 1536)
+    column_part(X2, 512)
+    column_part(Y2, 1024)
+    ring_pass(OUT, HALF)
+    column_part(Z2, 1792)
+    ring_pass(X1, 0)
+    column_part(X2, 768)
+    ring_pass(Y1, 256)
+    column_part(Y2, 1280)
+    ring_pass(Z2, 1536)
+    loss_next(0)
+    loss_send(1)
+    grad_normed(1 - me.core, gns, 0)
+    ring_pass(X2, 512)
+    grad_normed(1 - me.core, gns, 1)
+    ring_pass(Y2, 1024)
+    ring_pass(Z2, 1792)
+    advance(OUT, 0)
+    grad_normed(1 - me.core, gns, 2)
+    ring_pass(X2, 768)
+    grad_normed(1 - me.core, gns, 3)
     gn = [c.send(gns.at[:, i], gnr.at[:, i], r["gn_ss"].at[i], r["gn_rs"].at[i], me.core_peer()) for i in range(4)]
-    for k in (OUT, X1, Y1):
+    ring_pass(Y2, 1280)
+    for k in (X1, Y1):
         advance(k, 0)
     loss_next(1)
     loss_send(2)
-    grad_normed(me.core, gno)
+    for n in range(4):
+        grad_normed(me.core, gno, n)
+    advance(OUT, 1)
     norm_back(0)
     norm_back(1)
-    for k in (OUT, X1, Y1):
+    for k in (X1, Y1):
         advance(k, 1)
+    for k in (Z2, X2, Y2):
+        advance(k, 0)
+    out_stage(0, 0)
+    out_stage(1, 0)
     loss_next(2)
     loss_send(3)
     norm_back(2)
     norm_back(3)
     near = rim_send(rim_s.at[1 - me.xh], rim_r.at[0], 0, me.peer("x", 2))
     far = rim_send(rim_s.at[me.xh], rim_r.at[1], 1, me.peer("z", -me.turn))
-    out_stage(0, 0)
-    out_stage(1, 0)
     finish(X1)
     finish(Y1)
-    for k in (Z2, X2, Y2):
-        advance(k, 0)
-    far.wait_recv()
-    far = rim_send(rim_r.at[1], rim_r.at[2], 2, me.peer("y", -me.turn))
     out_stage(0, 1)
     out_stage(1, 1)
     for k in (Z2, X2, Y2):
         advance(k, 1)
     far.wait_recv()
+    far = rim_send(rim_r.at[1], rim_r.at[2], 2, me.peer("y", -me.turn))
+    for k in (X1, Y1):
+        finish_pass(k)
+    out_stage(0, 2)
+    out_stage(1, 2)
+    far.wait_recv()
     carried = jnp.where(me.xh == 0, me.z == 3, me.z == 0)
     last = rim_send(rim_r.at[jnp.where(carried, 2, 1)], rim_r.at[3], 3, me.peer("x", 2))
-    out_stage(0, 2)
-    out_stage(1, 2)
     for k in (Z2, X2, Y2):
         finish(k)
-    for k in (X1, Y1):
-        finish_pass(k)
     loss_next(3)
     out_stage(0, 3)
     out_stage(1, 3)

time: 106 us -> 102 us (0.962)
  Pallas kernels: 105 us -> 101 us
    pallas_call x1, Pallas kernels: 102 us -> 97.3 us  [local(): pl.pallas_call(kernel, out_shape=(jax.ShapeDtypeStruct((8, 128), F32),) +...]
where the time goes in v3:
time: 102 us; the launch traced here: 101 us
  Pallas kernels  101 us (99%)
    pallas_call x1, Pallas kernels, local(): pl.pallas_call(kernel, out_shape=(jax.ShapeDtypeStruct((8, 128), F32),) +...  97.3 us
    pallas_call x1, Pallas kernels, local(): pl.pallas_call(hand_on, out_shape=(jax.ShapeDtypeStruct((1, 1), F32),) +...  3.2 us

profile of v3, /device:TPU:1, one launch (start us, length us, event | category | flops | bytes accessed | tf_op | source)
XLA Modules:
  0.0 101.3 jit_solution(2845779197960392269)
XLA Ops:
  0.6 97.3 %shard_map.120 = (f32[8,128]{1,0:T(8,128)}, f32[4,16,1024]{2,1,0:T(8,128)}, f32[32,4096]{1,0:T(8,128)}, f32[100,4096]{1,0:T(8,128)}) custom-call(bf16[4,16,1024]{2,1,0:T(8,128)(2,1)} %lat.1, s32[3,128]{1,0:T(4,128)} %eidx.1, f32[3,128]{1,0:T(4,128)} %ewt.1, s32[4]{0:T(128)} %seed.1, f32[64,1024]{1,0:T(8,128)} %ntab.1, bf16[32,4096]{1,0:T(8,128)(2,1)} %w_in.1, ...), custom_call_target="tpu_custom_call" | custom-call | tf_op jit(solution)/shard_map/pallas_call | solution.py:707
  98.0 3.2 %shard_map.121 = (f32[1,1]{1,0:T(1,128)}, f32[4,16,1024]{2,1,0:T(8,128)}, f32[32,4096]{1,0:T(8,128)}, f32[100,4096]{1,0:T(8,128)}) custom-call(f32[8,128]{1,0:T(8,128)} %get-tuple-element.12.loss, f32[4,16,1024]{2,1,0:T(8,128)} %get-tuple-element.13.gl, f32[32,4096]{1,0:T(8,128)} %get-tuple-element.14.gwi, f32[100,4096]{1,0:T(8,128)} %get-tuple-element.15.gwo), custom_call_target="tpu_custom_call" | custom-call | tf_op jit(solution)/shard_map/pallas_call | solution.py:717

commit v4 on v3

--- a/solution.py
+++ b/solution.py
@@ -74,7 +74,6 @@
     gnr=pltpu.VMEM((4, 4, 32, LAT), BF16),
     rim_s=pltpu.VMEM((2, 16, LAT), F32),
     rim_r=pltpu.VMEM((4, 16, LAT), F32),
-    gwo=pltpu.VMEM((VARS, 2 * HALF), F32),
     glat=pltpu.VMEM((4, 16, LAT), F32),
     out_sem=DMA((6,)),
     loss_s=pltpu.VMEM((4, 8, 128), F32),
@@ -116,20 +115,28 @@
     def __init__(self):
         m, s = lax.axis_index("member"), lax.axis_index("space")
         self.m, self.s = m, s
-        self.xl, self.core = m // 2, m % 2
-        self.y, self.z, self.xh = s // 8, (s // 2) % 4, s % 2
+        self.xl, self.core = lax.div(m, 2), lax.rem(m, 2)
+        self.y, self.z, self.xh = lax.div(s, 8), lax.rem(lax.div(s, 2), 4), lax.rem(s, 2)
         self.x = self.xh * 2 + self.xl
         self.turn = 1 - 2 * self.xh
+        self.steps = {(a, 0): getattr(self, a) for a in "yzx"}
+        self.peers = {}
+        for a in "yzx":
+            for k in (1, 2, 3):
+                self.steps[a, k] = lax.rem(self.steps[a, 0] + k, 4)
+                self.peers[a, k] = self.device(**{b: self.steps[b, k if a == b else 0] for b in "yzx"})
 
     def device(self, y, z, x):
-        return ((x % 2) * 2 + self.core, (y * 4 + z) * 2 + x // 2)
-
-    def at(self, axis):
-        return getattr(self, axis)
+        return (lax.rem(x, 2) * 2 + self.core, (y * 4 + z) * 2 + lax.div(x, 2))
+
+    def at(self, axis, step=0):
+        return self.steps[axis, step]
 
     def peer(self, axis, step):
+        if isinstance(step, int):
+            return self.peers[axis, step]
         q = dict(y=self.y, z=self.z, x=self.x)
-        q[axis] = (q[axis] + step) % 4
+        q[axis] = lax.rem(q[axis] + step + 4, 4)
         return self.device(**q)
 
     def core_peer(self):
@@ -137,9 +144,6 @@
 
     def pair_peer(self):
         return ((1 - self.xl) * 2 + self.core, self.s)
-
-    def cross_peer(self):
-        return ((1 - self.xl) * 2 + 1 - self.core, self.s)
 
 
 class Copies:
@@ -173,7 +177,7 @@
     col0 = pl.multiple_of(me.core * HALF, 128)
 
     friends = [me.peer(a, k) for a in "yzx" for k in (1, 2, 3)]
-    friends += [me.core_peer(), me.cross_peer()]
+    friends.append(me.core_peer())
     barrier = pltpu.get_barrier_semaphore()
     for d in friends:
         pl.semaphore_signal(barrier, inc=1, device_id=d, device_id_type=MESH)
@@ -410,7 +414,7 @@
 
     def ring_start(k, c0):
         axis = ORDERS[k][0]
-        opposite = (me.at(axis) + 2) % 4
+        opposite = me.at(axis, 2)
         slot = c0 // 256
         flight[c0] = []
         for i in range(2):
@@ -429,7 +433,7 @@
         passed = []
         for i in range(2):
             flight[c0][i].wait_recv()
-            there = (me.at(axis) + 1 + 2 * i) % 4
+            there = me.at(axis, 1 + 2 * i)
             cols = slice(c0 + 128 * i, c0 + 128 * i + 128)
             for v in range(4):
                 index = [v, slice(None)]
@@ -453,7 +457,7 @@
         src, dst = ((sb2, rb2), (sb3, rb3))[stage - 1]
         flight[(k, stage)] = []
         for i in (2, 1, 3):
-            there = (me.at(axis) + i) % 4
+            there = me.at(axis, i)
             flight[(k, stage)].append(
                 c.send(
                     src.at[pick(axis, axes, there, cols)],
@@ -663,15 +667,7 @@
     for k in (Z2, X2, Y2):
         finish_pass(k)
     oc.wait_recv()
-    gwo = r["gwo"]
-    for core in range(2):
-        for b in range(56):
-            vg, hg = b // 8, b % 8
-            rows = min(16, VARS - 16 * vg)
-            block = obuf[core, b // 16, (b // 4) % 4, b % 4].astype(F32) * (1.0 / SCALE)
-            at = core * HALF + 256 * hg
-            gwo[16 * vg : 16 * vg + rows, at : at + 256] = block[0:rows]
-    leave.append(pltpu.make_async_copy(gwo, gwo_o, r["out_sem"].at[1]))
+    leave.append(pltpu.make_async_copy(obuf, gwo_o, r["out_sem"].at[1]))
     leave[1].start()
     for k in finals:
         arrive(finals[k])
@@ -692,7 +688,13 @@
     loss_o[0, 0] = jnp.sum(loss[...]) * (1.0 / POINTS)
     gl_o[...] = gl[...]
     gwi_o[...] = gwi[...]
-    gwo_o[...] = gwo[...]
+    for core in range(2):
+        for b in range(56):
+            vg, hg = b // 8, b % 8
+            rows = min(16, VARS - 16 * vg)
+            block = gwo[core, b // 16, (b // 4) % 4, b % 4].astype(F32) * (1.0 / SCALE)
+            at = core * HALF + 256 * hg
+            gwo_o[16 * vg : 16 * vg + rows, at : at + 256] = block[0:rows]
 
 
 def local(latent, edge_index, edge_weight, noise_seed, noise_table, w_in, w_out, target, area_weight):
@@ -702,11 +704,11 @@
     grads = (
         jax.ShapeDtypeStruct((4, 16, LAT), F32),
         jax.ShapeDtypeStruct((32, 2 * HALF), F32),
-        jax.ShapeDtypeStruct((VARS, 2 * HALF), F32),
     )
+    blocks = jax.ShapeDtypeStruct((2, 4, 4, 4, 16, 256), BF16)
     made = pl.pallas_call(
         kernel,
-        out_shape=(jax.ShapeDtypeStruct((8, 128), F32),) + grads,
+        out_shape=(jax.ShapeDtypeStruct((8, 128), F32),) + grads + (blocks,),
         in_specs=[vmem, vmem, vmem, smem] + [vmem] * 5,
         out_specs=(vmem,) + (anywhere,) * 3,
         scratch_shapes=list(SCRATCH.values()),
@@ -716,7 +718,7 @@
     )(latent, edge_index, edge_weight, noise_seed, noise_table, w_in, w_out, target, area_weight.reshape(1, -1))
     loss, grad_latent, grad_in, grad_out = pl.pallas_call(
         hand_on,
-        out_shape=(jax.ShapeDtypeStruct((1, 1), F32),) + grads,
+        out_shape=(jax.ShapeDtypeStruct((1, 1), F32),) + grads + (jax.ShapeDtypeStruct((VARS, 2 * HALF), F32),),
         in_specs=[vmem] * 4,
         out_specs=(smem,) + (vmem,) * 3,
     )(*made)

time: 102 us -> 101 us (level)
  no operation moved by 1% of the time
where the time goes in v4:
time: 101 us
  Pallas kernels  100 us (99%)
    pallas_call x1, Pallas kernels, local(): pl.pallas_call(kernel, out_shape=(jax.ShapeDtypeStruct((8, 128), F32),) +...  97.2 us
    pallas_call x1, Pallas kernels, local(): pl.pallas_call(hand_on, out_shape=(jax.ShapeDtypeStruct((1, 1), F32),) +...  2.97 us

profile of v4, /device:TPU:1, one launch (start us, length us, event | category | flops | bytes accessed | tf_op | source)
XLA Modules:
  0.0 101.0 jit_solution(5001675898350471175)
XLA Ops:
  0.6 97.2 %shard_map.120 = (f32[8,128]{1,0:T(8,128)}, f32[4,16,1024]{2,1,0:T(8,128)}, f32[32,4096]{1,0:T(8,128)}, bf16[2,4,4,4,16,256]{5,4,3,2,1,0:T(8,128)(2,1)}) custom-call(bf16[4,16,1024]{2,1,0:T(8,128)(2,1)} %lat.1, s32[3,128]{1,0:T(4,128)} %eidx.1, f32[3,128]{1,0:T(4,128)} %ewt.1, s32[4]{0:T(128)} %seed.1, f32[64,1024]{1,0:T(8,128)} %ntab.1, ...), custom_call_target="tpu_custom_call" | custom-call | tf_op jit(solution)/shard_map/pallas_call | solution.py:709
  97.9 3.0 %shard_map.121 = (f32[1,1]{1,0:T(1,128)}, f32[4,16,1024]{2,1,0:T(8,128)}, f32[32,4096]{1,0:T(8,128)}, f32[100,4096]{1,0:T(8,128)}) custom-call(f32[8,128]{1,0:T(8,128)} %get-tuple-element.12.loss, f32[4,16,1024]{2,1,0:T(8,128)} %get-tuple-element.13.gl, f32[32,4096]{1,0:T(8,128)} %get-tuple-element.14.gwi, bf16[2,4,4,4,16,256]{5,4,3,2,1,0:T(8,128)(2,1)} %get-tuple-element.15.gwo), custom_call_target="tpu_custom_call" | custom-call | tf_op jit(solution)/shard_map/pallas_call | solution.py:719

commit v5 on v4

--- a/solution.py
+++ b/solution.py
@@ -620,11 +620,12 @@
         grad_normed(me.core, gno, n)
     advance(OUT, 1)
     norm_back(0)
+    advance(Z2, 0)
     norm_back(1)
+    for k in (X2, Y2):
+        advance(k, 0)
     for k in (X1, Y1):
         advance(k, 1)
-    for k in (Z2, X2, Y2):
-        advance(k, 0)
     out_stage(0, 0)
     out_stage(1, 0)
     loss_next(2)

time: 101 us -> 101 us (level)
  no operation moved by 1% of the time
where the time goes in v5:
time: 101 us
  Pallas kernels  101 us (100%)
    pallas_call x1, Pallas kernels, local(): pl.pallas_call(kernel, out_shape=(jax.ShapeDtypeStruct((8, 128), F32),) +...  97.5 us
    pallas_call x1, Pallas kernels, local(): pl.pallas_call(hand_on, out_shape=(jax.ShapeDtypeStruct((1, 1), F32),) +...  2.97 us

profile of v5, /device:TPU:1, one launch (start us, length us, event | category | flops | bytes accessed | tf_op | source)
XLA Modules:
  0.0 101.3 jit_solution(2102741536815395188)
XLA Ops:
  0.6 97.5 %shard_map.120 = (f32[8,128]{1,0:T(8,128)}, f32[4,16,1024]{2,1,0:T(8,128)}, f32[32,4096]{1,0:T(8,128)}, bf16[2,4,4,4,16,256]{5,4,3,2,1,0:T(8,128)(2,1)}) custom-call(bf16[4,16,1024]{2,1,0:T(8,128)(2,1)} %lat.1, s32[3,128]{1,0:T(4,128)} %eidx.1, f32[3,128]{1,0:T(4,128)} %ewt.1, s32[4]{0:T(128)} %seed.1, f32[64,1024]{1,0:T(8,128)} %ntab.1, ...), custom_call_target="tpu_custom_call" | custom-call | tf_op jit(solution)/shard_map/pallas_call | solution.py:710
  98.2 3.0 %shard_map.121 = (f32[1,1]{1,0:T(1,128)}, f32[4,16,1024]{2,1,0:T(8,128)}, f32[32,4096]{1,0:T(8,128)}, f32[100,4096]{1,0:T(8,128)}) custom-call(f32[8,128]{1,0:T(8,128)} %get-tuple-element.12.loss, f32[4,16,1024]{2,1,0:T(8,128)} %get-tuple-element.13.gl, f32[32,4096]{1,0:T(8,128)} %get-tuple-element.14.gwi, bf16[2,4,4,4,16,256]{5,4,3,2,1,0:T(8,128)(2,1)} %get-tuple-element.15.gwo), custom_call_target="tpu_custom_call" | custom-call | tf_op jit(solution)/shard_map/pallas_call | solution.py:720
